TPU v7x, 128 devices: a whole 4x4x4 slice. The times are simulated.
128 devices in a mesh: dp: 32 (over y, z, core), tensor: 4 (over x).
Axes of the slice: x: 4, y: 4, z: 4, core: 2. Of those that a mesh axis runs over, the one named last changes fastest.
Arguments:
- queries: bfloat16 [4096, 4096], P('dp', 'tensor'), may hold values from -120 to 120
- token_keys: bfloat16 [4096, 512], P('dp', 'tensor'), may hold values from -4 to 4
- token_values: bfloat16 [4096, 512], P('dp', 'tensor'), may hold values from -4 to 4
- cached_key_rows: bfloat16 [4096, 256, 512], P('dp', None, 'tensor'), may hold values from -4 to 4
- cached_value_rows: bfloat16 [4096, 256, 512], P('dp', None, 'tensor'), may hold values from -4 to 4
- cache_length: int32 [4096], P('dp'), may hold values from 2 to 256, as said below
- output_projection: bfloat16 [4096, 8192], P(None, 'tensor'), may hold values from -0.75 to 0.75
- request_adapter: int32 [4096], P('dp'), may hold values from 0 to 31, as said below
- adapter_table_row: int32 [32], replicated, may hold values from 0 to 31, each once
- adapter_down_weight: bfloat16 [32, 64, 4096], P('dp', None, 'tensor'), may hold values from -0.75 to 0.75
- adapter_up_weight: bfloat16 [32, 64, 8192], P('dp', None, 'tensor'), may hold values from -0.75 to 0.75
Outputs:
- mixed: bfloat16 [4096, 8192], P('dp', 'tensor')
Inputs may be any that keep to these rules, and one draw needn't show every extreme that they name: `cache_length`: at least one request has exactly 256 used positions. `request_adapter`: among the 128 requests of one index of dp no adapter id occurs more than 8 times; in every draw one adapter id occurs exactly 8 times on every index of dp. `adapter_table_row`: each row 0 to 31 is named once.
All inputs are finite; a program needn't handle non-finite values.
Results may differ from a plain program's by a relative error of at most 0.01.
Values may be sent and summed in bfloat16 or wider, within the bound.
No kernel may reach another device: no remote copies, remote signals or barrier semaphores. Data moves between devices by JAX's collectives and lax.ppermute only.
A program may use at most 128 MiB of HBM per device.

v0:
```python
import math

import jax
import jax.numpy as jnp
from jax import lax
from jax.sharding import PartitionSpec as P

HEADS = 32
KV_HEADS = 4
HEAD_DIM = 128


def attend(queries, token_keys, token_values, cached_key_rows, cached_value_rows, cache_length):
    requests = queries.shape[0]
    kv_local = token_keys.shape[1] // HEAD_DIM
    per_group = HEADS // KV_HEADS
    positions = cached_key_rows.shape[1]
    score_scale = 1.0 / math.sqrt(HEAD_DIM)
    query_heads = queries.reshape(requests, kv_local, per_group, HEAD_DIM)
    key_blocks = cached_key_rows.reshape(requests, positions, kv_local, HEAD_DIM)
    value_blocks = cached_value_rows.reshape(requests, positions, kv_local, HEAD_DIM)
    fresh_keys = token_keys.reshape(requests, kv_local, HEAD_DIM)
    fresh_values = token_values.reshape(requests, kv_local, HEAD_DIM)
    cached_score = (
        jnp.einsum("rkgd,rpkd->rkgp", query_heads, key_blocks, preferred_element_type=jnp.float32)
        * score_scale
    )
    fresh_score = (
        jnp.einsum("rkgd,rkd->rkg", query_heads, fresh_keys, preferred_element_type=jnp.float32)
        * score_scale
    )
    in_cache = (jnp.arange(positions, dtype=jnp.int32)[None, :] < cache_length[:, None])[
        :, None, None, :
    ]
    row_max = jnp.maximum(
        jnp.max(jnp.where(in_cache, cached_score, -jnp.inf), axis=-1), fresh_score
    )
    cached_weight = jnp.where(in_cache, jnp.exp(cached_score - row_max[..., None]), 0.0)
    fresh_weight = jnp.exp(fresh_score - row_max)
    weight_sum = jnp.sum(cached_weight, axis=-1) + fresh_weight
    combined = jnp.einsum(
        "rkgp,rpkd->rkgd",
        cached_weight.astype(jnp.bfloat16),
        value_blocks,
        preferred_element_type=jnp.float32,
    )
    combined = combined + jnp.einsum(
        "rkg,rkd->rkgd",
        fresh_weight.astype(jnp.bfloat16),
        fresh_values,
        preferred_element_type=jnp.float32,
    )
    return (
        (combined / weight_sum[..., None])
        .reshape(requests, kv_local * per_group * HEAD_DIM)
        .astype(jnp.bfloat16)
    )


def on_device(
    queries,
    token_keys,
    token_values,
    cached_key_rows,
    cached_value_rows,
    cache_length,
    output_projection,
    request_adapter,
    adapter_table_row,
    adapter_down_weight,
    adapter_up_weight,
):
    attention_output = attend(
        queries, token_keys, token_values, cached_key_rows, cached_value_rows, cache_length
    )
    requests = attention_output.shape[0]
    feature_cols = attention_output.shape[1]
    projected = jnp.dot(
        lax.all_gather(attention_output, "tensor", axis=1, tiled=True),
        output_projection,
        preferred_element_type=jnp.float32,
    )
    every_adapter = adapter_table_row.shape[0]
    table_capacity = 2 * requests // every_adapter
    matches = request_adapter[:, None] == jnp.arange(every_adapter, dtype=jnp.int32)[None, :]
    slot_of = jnp.sum(jnp.where(matches, adapter_table_row[None, :], 0), axis=1)
    request_order = jnp.arange(requests, dtype=jnp.int32)
    earlier = (slot_of[:, None] == slot_of[None, :]) & (
        request_order[:, None] > request_order[None, :]
    )
    position = slot_of * table_capacity + jnp.sum(earlier.astype(jnp.int32), axis=1)
    placing = (
        jnp.arange(every_adapter * table_capacity, dtype=jnp.int32)[:, None] == position[None, :]
    ).astype(jnp.bfloat16)
    buffer_rows = jnp.dot(placing, attention_output, preferred_element_type=jnp.float32).astype(
        jnp.bfloat16
    )
    table_down, table_up = (
        lax.all_gather(adapter_down_weight, "dp", axis=0, tiled=True),
        lax.all_gather(adapter_up_weight, "dp", axis=0, tiled=True),
    )
    grouped = buffer_rows.reshape(every_adapter, table_capacity, feature_cols)
    rank_terms = jnp.einsum("acw,arw->acr", grouped, table_down, preferred_element_type=jnp.float32)
    low_rank_state = lax.psum(rank_terms, "tensor").astype(jnp.bfloat16)
    adapter_deltas = jnp.einsum(
        "acr,ard->acd", low_rank_state, table_up, preferred_element_type=jnp.float32
    ).astype(jnp.bfloat16)
    adapter_deltas = adapter_deltas.reshape(
        every_adapter * table_capacity, adapter_up_weight.shape[2]
    )
    returned = jnp.einsum("sr,sd->rd", placing, adapter_deltas, preferred_element_type=jnp.float32)
    return (projected + returned).astype(jnp.bfloat16)


def solution(mesh):
    in_specs = (
        P("dp", "tensor"),
        P("dp", "tensor"),
        P("dp", "tensor"),
        P("dp", None, "tensor"),
        P("dp", None, "tensor"),
        P("dp"),
        P(None, "tensor"),
        P("dp"),
        P(),
        P("dp", None, "tensor"),
        P("dp", None, "tensor"),
    )
    out_specs = P("dp", "tensor")
    return jax.shard_map(
        on_device, mesh=mesh, in_specs=in_specs, out_specs=out_specs, check_vma=False
    )
```

profile of v0, /device:TPU:0, one launch (start us, length us, event | category | flops | bytes accessed | tf_op | source)
XLA Modules:
  0.0 159.8 jit_solution(15225295024856014704)
XLA Ops:
  6.5 0.0 copy-start
  6.5 0.0 all-gather.4.cloned.1.call-start
  6.5 0.9 iota_compare_fusion.4
  7.4 1.4 copy.14
  8.9 0.0 copy-done
  8.9 0.3 fusion.17
  9.1 5.7 %select_reduce_fusion = (f32[128,8]{1,0:T(8,128)S(1)}, f32[128,8,256]{2,1,0:T(8,128)S(1)}) fusion(pred[128,256]{1,0:T(8,128)(4,1)S(1)} %iota_compare_fusion.4, bf16[128,8,128]{2,1,0:T(8,128)(2,1)S(1)} %bitcast.32, bf16[128,256,128]{2,1,0:T(8,128)(2,1)} %param.14), kind=kOutput, calls=%fused_computation.11 | convolution fusion | flops 67894272 | bytes 9736192 | tf_op jit(solution)/shard_map/rkgd,rpkd->rkgp/dot_general | solution.py:25
  14.9 0.4 fusion.5
  15.4 1.3 fusion.4
  16.7 0.8 copy.21
  17.4 0.0 all-gather.4.cloned.1.call-update
  17.5 0.0 all-gather.6.cloned.1.call-start
  17.5 0.7 all-gather.6.cloned.1.call-update
  18.2 0.0 all-gather.8.cloned.1.call-start
  18.3 0.7 all-gather.8.cloned.1.call-update
  19.0 0.1 select_reduce_fusion.1
  19.1 0.2 convert_reduce_fusion
  19.3 24.8 %all-gather.4.cloned.1.call-done = bf16[128,4096]{1,0:T(8,128)(2,1)} async-done(((bf16[128,1024]{1,0:T(8,128)(2,1)}), bf16[128,4096]{1,0:T(8,128)(2,1)}) %all-gather.4.cloned.1.call-update) | async-done | bytes 1048592 | tf_op jit(solution)/shard_map/all_gather | solution.py:79
  44.0 8.4 %fusion.22 = f32[128,2048]{1,0:T(8,128)S(1)} fusion(bf16[128,4096]{1,0:T(8,128)(2,1)} %all-gather.4.cloned.1.call-done, bf16[4096,2048]{1,0:T(8,128)(2,1)} %param.17), kind=kOutput, calls=%fused_computation.37 | convolution fusion | flops 2147483648 | bytes 18874368 | tf_op jit(solution)/shard_map/dot_general | solution.py:78
  52.5 40.6 %all-gather.6.cloned.1.call-done = bf16[32,64,1024]{2,1,0:T(8,128)(2,1)} async-done(((bf16[1,64,1024]{2,1,0:T(8,128)(2,1)}), bf16[32,64,1024]{2,1,0:T(8,128)(2,1)}) %all-gather.6.cloned.1.call-update) | async-done | bytes 4194320 | tf_op jit(solution)/shard_map/all_gather | solution.py:99
  93.1 3.5 %fusion.7 = f32[32,8,64]{2,1,0:T(8,128)S(1)} fusion(bf16[32,64,1024]{2,1,0:T(8,128)(2,1)} %all-gather.6.cloned.1.call-done, s32[128]{0:T(128)S(1)} %multiply_add_fusion, bf16[16,8,8,128]{3,2,1,0:T(8,128)(2,1)S(1)} %bitcast.30), kind=kOutput, calls=%fused_computation.14 | convolution fusion | flops 100958208 | bytes 4522496 | tf_op jit(solution)/shard_map/acw,arw->acr/dot_general | solution.py:103
  96.6 18.3 %psum.7 = bf16[32,8,64]{2,1,0:T(8,128)(2,1)S(1)} all-reduce(f32[32,8,64]{2,1,0:T(8,128)S(1)} %fusion.7), channel_id=1, replica_groups=mesh['dp'=32,'tensor'=4] {'tensor'}, use_global_device_ids=true, to_apply=%region_4.5 | all-reduce | flops 16384 | bytes 98304 | tf_op jit(solution)/shard_map/psum | solution.py:104
  114.9 32.7 %all-gather.8.cloned.1.call-done = bf16[32,64,2048]{2,1,0:T(8,128)(2,1)} async-done(((bf16[1,64,2048]{2,1,0:T(8,128)(2,1)}), bf16[32,64,2048]{2,1,0:T(8,128)(2,1)}) %all-gather.8.cloned.1.call-update) | async-done | bytes 8388624 | tf_op jit(solution)/shard_map/all_gather | solution.py:100
  147.7 5.6 %fusion.1 = bf16[128,2048]{1,0:T(8,128)(2,1)} fusion(f32[128,2048]{1,0:T(8,128)S(1)} %fusion.22, bf16[32,64,2048]{2,1,0:T(8,128)(2,1)} %all-gather.8.cloned.1.call-done, bf16[32,8,64]{2,1,0:T(8,128)(2,1)S(1)} %psum.7, s32[128]{0:T(128)S(1)} %multiply_add_fusion), kind=kOutput, calls=%fused_computation.3 | convolution fusion | flops 202407936 | bytes 9994752 | tf_op jit(solution)/shard_map/sr,sd->rd/dot_general | solution.py:111
  (12 shorter events, 0.1 us)
Async XLA Ops:
  6.5 2.3 %copy-start = (bf16[128,128]{1,0:T(8,128)(2,1)S(1)}, bf16[128,128]{1,0:T(8,128)(2,1)}, u32[]{:S(2)}) copy-start(bf16[128,128]{1,0:T(8,128)(2,1)} %param.12) | copy-start | bytes 98308
  6.5 8.8 %copy-start.1 = (bf16[128,128]{1,0:T(8,128)(2,1)S(1)}, bf16[128,128]{1,0:T(8,128)(2,1)}, u32[]{:S(2)}) copy-start(bf16[128,128]{1,0:T(8,128)(2,1)} %param.13) | copy-start | bytes 98308
  6.5 37.5 %all-gather.4.cloned.1.call-start = ((), (), s32[]{:S(2)}) async-start(), calls=%async_computation | async-start | bytes 1310720 | tf_op jit(solution)/shard_map/all_gather | solution.py:79
  6.5 8.8 %copy-start.2 = (bf16[128,256,128]{2,1,0:T(8,128)(2,1)S(1)}, bf16[128,256,128]{2,1,0:T(8,128)(2,1)}, u32[]{:S(2)}) copy-start(bf16[128,256,128]{2,1,0:T(8,128)(2,1)} %param.15) | copy-start | bytes 25165828
  14.9 4.1 %copy-start.3 = (s32[32]{0:T(128)S(1)}, s32[32]{0:T(128)}, u32[]{:S(2)}) copy-start(s32[32]{0:T(128)} %param.19) | copy-start | bytes 388
  14.9 4.1 %copy-start.4 = (s32[128]{0:T(128)S(1)}, s32[128]{0:T(128)}, u32[]{:S(2)}) copy-start(s32[128]{0:T(128)} %param.18) | copy-start | bytes 1540
  17.5 75.6 %all-gather.6.cloned.1.call-start = ((), (), s32[]{:S(2)}) async-start(), calls=%async_computation.1 | async-start | bytes 4325376 | tf_op jit(solution)/shard_map/all_gather | solution.py:99
  18.2 129.4 %all-gather.8.cloned.1.call-start = ((), (), s32[]{:S(2)}) async-start(), calls=%async_computation.2 | async-start | bytes 8650752 | tf_op jit(solution)/shard_map/all_gather | solution.py:100
Sparse Core Ops, SparseCore 0:
  17.6 26.3 all-gather.3
  46.3 46.7 all-gather.5
  95.3 52.2 all-gather.7
where the time goes:
time: 161 us; the launch traced here: 160 us
  waiting for transfers between devices  99.5 us (62%)
  matrix products  24.9 us (15%)
  blocking collectives  18.3 us (11%)
  between operations  13.2 us (8%)
  local copies, waits for them, and re-layouts  2.18 us (1%)
  other arithmetic  1.61 us (1%)
    all_gather x1, waiting for transfers between devices, on_device(): lax.all_gather(adapter_down_weight, 'dp', axis=0, tiled=True)  40.6 us
    all_gather x1, waiting for transfers between devices, on_device(): lax.all_gather(adapter_up_weight, 'dp', axis=0, tiled=True)  32.7 us
    all_gather x1, waiting for transfers between devices, on_device(): lax.all_gather(attention_output, 'tensor', axis=1, tiled=True)  24.8 us
    psum x1, blocking collectives, on_device(): low_rank_state = lax.psum(rank_terms, 'tensor').astype(jnp.bfloat16)  18.3 us
    dot_general x1, matrix products, on_device(): jnp.dot(lax.all_gather(attention_output, 'tensor', axis=1, tiled=True), o...  8.44 us
    dot_general x1, matrix products, attend(): jnp.einsum('rkgd,rpkd->rkgp', query_heads, key_blocks, preferred_element_...  5.74 us
    dot_general x1, matrix products, on_device(): jnp.einsum('sr,sd->rd', placing, adapter_deltas, preferred_element_type=j...  5.62 us
    dot_general x1, matrix products, on_device(): jnp.einsum('acw,arw->acr', grouped, table_down, preferred_element_type=jn...  3.54 us
  transfers between devices with their start and end apart: 3, of which 3 were waited for; matrix products, arithmetic and copies ran while one was open for 8% of the time, Pallas kernels for 0%

commit v1 on v0

v1 whole, which is shorter than its diff:
```python
import math

import jax
import jax.numpy as jnp
from jax import lax
from jax.sharding import PartitionSpec as P

HEADS = 32
KV_HEADS = 4
HEAD_DIM = 128
CAP = 8
Z_CHIPS = 4
CORES = 2
RING = 4


def attend(queries, token_keys, token_values, cached_key_rows, cached_value_rows, cache_length):
    requests = queries.shape[0]
    per_group = HEADS // KV_HEADS
    positions = cached_key_rows.shape[1]
    score_scale = 1.0 / math.sqrt(HEAD_DIM)
    query_heads = queries.reshape(requests, per_group, HEAD_DIM)
    cached_score = (
        jnp.einsum("rgd,rpd->rgp", query_heads, cached_key_rows, preferred_element_type=jnp.float32)
        * score_scale
    )
    fresh_score = (
        jnp.einsum("rgd,rd->rg", query_heads, token_keys, preferred_element_type=jnp.float32)
        * score_scale
    )
    in_cache = (jnp.arange(positions, dtype=jnp.int32)[None, :] < cache_length[:, None])[:, None, :]
    row_max = jnp.maximum(
        jnp.max(jnp.where(in_cache, cached_score, -jnp.inf), axis=-1), fresh_score
    )
    cached_weight = jnp.where(in_cache, jnp.exp(cached_score - row_max[..., None]), 0.0)
    fresh_weight = jnp.exp(fresh_score - row_max)
    weight_sum = jnp.sum(cached_weight, axis=-1) + fresh_weight
    combined = jnp.einsum(
        "rgp,rpd->rgd",
        cached_weight.astype(jnp.bfloat16),
        cached_value_rows,
        preferred_element_type=jnp.float32,
    )
    combined = combined + jnp.einsum(
        "rg,rd->rgd",
        fresh_weight.astype(jnp.bfloat16),
        token_values,
        preferred_element_type=jnp.float32,
    )
    return (
        (combined / weight_sum[..., None])
        .reshape(requests, per_group * HEAD_DIM)
        .astype(jnp.bfloat16)
    )


def swap_tensor(value, k):
    return lax.ppermute(value, "tensor", [(i, i ^ k) for i in range(RING)])


def swap_dp(value, k):
    return lax.ppermute(value, "dp", [(i, i ^ k) for i in range(RING * Z_CHIPS * CORES)])


def on_device(
    queries,
    token_keys,
    token_values,
    cached_key_rows,
    cached_value_rows,
    cache_length,
    output_projection,
    request_adapter,
    adapter_table_row,
    adapter_down_weight,
    adapter_up_weight,
):
    bf16, f32 = jnp.bfloat16, jnp.float32
    requests = queries.shape[0]
    features = queries.shape[1]
    rank = adapter_down_weight.shape[1]
    columns = output_projection.shape[1]
    owned = Z_CHIPS * CORES
    here = lax.axis_index("dp")
    mine = lax.axis_index("tensor")

    weights = jnp.concatenate([adapter_down_weight[0], adapter_up_weight[0]], axis=1)
    over_z = jnp.stack([weights] + [swap_dp(weights, k * CORES) for k in range(1, Z_CHIPS)])
    table = jnp.stack([over_z, swap_dp(over_z, 1)], axis=1).reshape(owned, rank, features + columns)
    table_down, table_up = table[:, :, :features], table[:, :, features:]

    attended = attend(
        queries, token_keys, token_values, cached_key_rows, cached_value_rows, cache_length
    )

    every_adapter = adapter_table_row.shape[0]
    matches = request_adapter[:, None] == jnp.arange(every_adapter, dtype=jnp.int32)[None, :]
    slot_of = jnp.sum(jnp.where(matches, adapter_table_row[None, :], 0), axis=1)
    order = jnp.arange(requests, dtype=jnp.int32)
    earlier = (slot_of[:, None] == slot_of[None, :]) & (order[:, None] > order[None, :])
    position = (slot_of ^ here) * CAP + jnp.sum(earlier.astype(jnp.int32), axis=1)
    placing = (
        jnp.arange(every_adapter * CAP, dtype=jnp.int32)[:, None] == position[None, :]
    ).astype(bf16)
    placed = jnp.dot(placing, attended, preferred_element_type=f32).astype(bf16)
    placed = placed.reshape(RING, owned * CAP, features)
    routed = [placed[0]] + [swap_dp(placed[m], m * owned) for m in range(1, RING)]

    pieces = [attended] + [swap_tensor(attended, k) for k in range(1, RING)]
    gathered = jnp.zeros((requests, RING * features), bf16)
    for k, piece in enumerate(pieces):
        gathered = lax.dynamic_update_slice(gathered, piece, (0, (mine ^ k) * features))
    projected = jnp.dot(gathered, output_projection, preferred_element_type=f32)

    grouped = jnp.stack(routed).reshape(RING, owned, CAP, features)
    partial = jnp.einsum("makw,arw->amkr", grouped, table_down, preferred_element_type=f32)
    partial = partial.reshape(2, owned * RING * CAP // 2, rank)
    partial = jnp.concatenate([partial[0], partial[1]], axis=1)
    total = partial
    for k in range(1, RING):
        total = total + swap_tensor(partial, k)
    low_rank = total.astype(bf16)
    low_rank = jnp.stack([low_rank[:, :rank], low_rank[:, rank:]]).reshape(owned, RING, CAP, rank)
    delta = jnp.einsum("amkr,ard->makd", low_rank, table_up, preferred_element_type=f32).astype(
        bf16
    )
    delta = delta.reshape(RING, owned * CAP, columns)
    back = [delta[0]] + [swap_dp(delta[m], m * owned) for m in range(1, RING)]
    returned = jnp.dot(placing.T, jnp.concatenate(back, axis=0), preferred_element_type=f32)
    return (projected + returned).astype(bf16)


def solution(mesh):
    in_specs = (
        P("dp", "tensor"),
        P("dp", "tensor"),
        P("dp", "tensor"),
        P("dp", None, "tensor"),
        P("dp", None, "tensor"),
        P("dp"),
        P(None, "tensor"),
        P("dp"),
        P(),
        P("dp", None, "tensor"),
        P("dp", None, "tensor"),
    )
    out_specs = P("dp", "tensor")
    return jax.shard_map(
        on_device, mesh=mesh, in_specs=in_specs, out_specs=out_specs, check_vma=False
    )
```

time: 161 us -> 77.4 us (0.48)
  waiting for transfers between devices: 99.5 us -> 24.1 us
  starting transfers between devices: 0.08 us -> 22.8 us
  blocking collectives: 18.3 us -> 0 us
  between operations: 13.2 us -> 0.32 us
  matrix products: 24.9 us -> 20.4 us
  local copies, waits for them, and re-layouts: 2.18 us -> 5.07 us
  other arithmetic: 1.61 us -> 4.32 us
    all_gather x3 -> x0, waiting for transfers between devices: 98.1 us -> none  [the longest x1 40.6 us: on_device(): lax.all_gather(adapter_down_weight, 'dp', axis=0, tiled=True)]
    ppermute x0 -> x16, waiting for transfers between devices: none -> 24.1 us  [the longest x10 22.3 us: swap_dp(): lax.ppermute(value, 'dp', [(i, i ^ k) for i in range(RING * Z_CHIPS * COR...]
    ppermute x0 -> x16, starting transfers between devices: none -> 22.8 us  [the longest x10 13.4 us: swap_dp(): lax.ppermute(value, 'dp', [(i, i ^ k) for i in range(RING * Z_CHIPS * COR...]
    psum x1 -> x0, blocking collectives: 18.3 us -> none  [on_device(): low_rank_state = lax.psum(rank_terms, 'tensor').astype(jnp.bfloat16)]
    dot_general x6 -> x8, matrix products: 24.9 us -> 20.4 us  [the longest x1 8.97 us: on_device(): projected = jnp.dot(gathered, output_projection, preferred_element_type=f32)]
    another operation x2 -> x6, other arithmetic: 0.03 us -> 2.81 us  [the longest x2 1.71 us: on_device(): jnp.stack([over_z, swap_dp(over_z, 1)], axis=1)]
    dynamic_update_slice x0 -> x4, local copies, waits for them, and re-layouts: none -> 2 us  [on_device(): lax.dynamic_update_slice(gathered, piece, (0, (mine ^ k) * features))]
  transfers between devices with their start and end apart: 3 -> 16, of which waited for: 3 -> 9; matrix products, arithmetic and copies ran while one was open for 8% -> 23% of each run, Pallas kernels for 0% -> 0%
where the time goes in v1:
time: 77.4 us; the launch traced here: 77.1 us
  waiting for transfers between devices  24.1 us (31%)
  starting transfers between devices  22.8 us (29%)
  matrix products  20.4 us (26%)
  local copies, waits for them, and re-layouts  5.07 us (7%)
  other arithmetic  4.32 us (6%)
    ppermute x10, waiting for transfers between devices, swap_dp(): lax.ppermute(value, 'dp', [(i, i ^ k) for i in range(RING * Z_CHIPS * COR...  22.3 us
    ppermute x10, starting transfers between devices, swap_dp(): lax.ppermute(value, 'dp', [(i, i ^ k) for i in range(RING * Z_CHIPS * COR...  13.4 us
    ppermute x6, starting transfers between devices, swap_tensor(): return lax.ppermute(value, 'tensor', [(i, i ^ k) for i in range(RING)])  9.38 us
    dot_general x1, matrix products, on_device(): projected = jnp.dot(gathered, output_projection, preferred_element_type=f32)  8.97 us
    dot_general x1, matrix products, attend(): jnp.einsum('rgd,rpd->rgp', query_heads, cached_key_rows, preferred_elemen...  5.88 us
    dot_general x1, matrix products, on_device(): jnp.einsum('amkr,ard->makd', low_rank, table_up, preferred_element_type=f32)  2.01 us
    dynamic_update_slice x4, local copies, waits for them, and re-layouts, on_device(): lax.dynamic_update_slice(gathered, piece, (0, (mine ^ k) * features))  2 us
    unnamed x18, local copies, waits for them, and re-layouts  1.8 us
  transfers between devices with their start and end apart: 16, of which 9 were waited for; matrix products, arithmetic and copies ran while one was open for 23% of the time, Pallas kernels for 0%

profile of v1, /device:TPU:0, one launch (start us, length us, event | category | flops | bytes accessed | tf_op | source)
XLA Modules:
  0.0 77.1 jit_solution(7948140971351543396)
XLA Ops:
  0.0 1.1 %fusion.35 = (bf16[1,64,3072]{2,1,0:T(8,128)(2,1)S(1)}, bf16[64,3072]{1,0:T(8,128)(2,1)S(1)}) fusion(bf16[64,2048]{1,0:T(8,128)(2,1)} %bitcast.87, bf16[64,1024]{1,0:T(8,128)(2,1)} %bitcast.88), kind=kLoop, calls=%fused_computation.71 | loop fusion | flops 786432 | bytes 1179648 | tf_op jit(solution)/shard_map/stack | solution.py:88
  1.1 4.2 %collective-permute-start.5 = (bf16[64,3072]{1,0:T(8,128)(2,1)S(1)}, bf16[64,3072]{1,0:T(8,128)(2,1)S(1)}, u32[]{:S(2)}, u32[]{:S(2)}) collective-permute-start(bf16[64,3072]{1,0:T(8,128)(2,1)S(1)} %get-tuple-element.16), channel_id=1, source_target_pairs={{0,24},{4,28},{8,16},{12,20},{16,8},{20,12},{24,0},{28,4},{32,56},... | collective-permute-start | bytes 1179656 | tf_op jit(solution)/shard_map/ppermute | solution.py:62
  7.0 1.0 %copy.26 = bf16[16,8,8,128]{3,2,1,0:T(8,128)(2,1)S(1)} copy(bf16[16,8,8,128]{3,1,2,0:T(8,128)(2,1)} %bitcast.84) | data formatting | bytes 524288
  8.3 5.9 %select_reduce_fusion = (f32[128,8]{1,0:T(8,128)S(1)}, f32[128,8,256]{2,1,0:T(8,128)S(1)}) fusion(pred[128,256]{1,0:T(8,128)(4,1)S(1)} %iota_compare_fusion.3, bf16[128,8,128]{2,1,0:T(8,128)(2,1)S(1)} %bitcast.78, bf16[128,256,128]{2,1,0:T(8,128)(2,1)} %param.14), kind=kOutput, calls=%fused_computation.23 | convolution fusion | flops 67894272 | bytes 9736192 | tf_op jit(solution)/shard_map/rgd,rpd->rgp/dot_general | solution.py:24
  14.6 8.2 %collective-permute-done.5 = bf16[64,3072]{1,0:T(8,128)(2,1)S(1)} collective-permute-done((bf16[64,3072]{1,0:T(8,128)(2,1)S(1)}, bf16[64,3072]{1,0:T(8,128)(2,1)S(1)}, u32[]{:S(2)}, u32[]{:S(2)}) %collective-permute-start.5) | collective-permute-done | bytes 393248 | tf_op jit(solution)/shard_map/ppermute | solution.py:62
  23.5 1.4 %fusion.36 = (bf16[4,1,64,3072]{3,2,0,1:T(8,128)(2,1)S(1)}, bf16[4,64,3072]{2,1,0:T(8,128)(2,1)}) fusion(bf16[1,64,3072]{2,1,0:T(8,128)(2,1)S(1)} %bitcast.79, bf16[1,64,3072]{2,1,0:T(8,128)(2,1)S(1)} %bitcast.80, bf16[1,64,3072]{2,1,0:T(8,128)(2,1)S(1)} %bitcast.81, bf16[1,64,3072]{2,1,0:T(8,128)(2,1)S(1)} %get-tuple-element.15), kind=kLoop, calls=%fused_computation.72 | loop fusion | flops 2359296 | bytes 4718592 | tf_op jit(solution)/shard_map/stack | solution.py:89
  25.1 1.3 %fusion.3 = bf16[128,8,128]{2,1,0:T(8,128)(2,1)S(1)} fusion(bf16[128,256,128]{2,1,0:T(8,128)(2,1)S(1)} %bitcast.91, f32[128,8,256]{2,1,0:T(8,128)S(1)} %get-tuple-element.24, f32[128,8]{1,0:T(8,128)S(1)} %multiply_maximum_fusion, pred[128,256]{1,0:T(8,128)(4,1)S(1)} %iota_compare_fusion.3, f32[128,8]{1,0:T(8,128)S(1)} %get-tuple-element.20, ...), kind=kOutput, calls=%fused_computation.11 | convolution fusion | flops 68419584 | bytes 9809920 | tf_op jit(solution)/shard_map/rgp,rpd->rgd/dot_general | solution.py:38
  27.1 1.5 %collective-permute-start = (bf16[128,1024]{1,0:T(8,128)(2,1)}, bf16[128,1024]{1,0:T(8,128)(2,1)}, u32[]{:S(2)}, u32[]{:S(2)}) collective-permute-start(bf16[128,1024]{1,0:T(8,128)(2,1)} %bitcast.69), channel_id=1, source_target_pairs={{0,1},{1,0},{2,3},{3,2},{4,5},{5,4},{6,7},{7,6},{8,9},{9,8},{10,11... | collective-permute-start | bytes 786440 | tf_op jit(solution)/shard_map/ppermute | solution.py:58
  28.6 2.7 %collective-permute-start.1 = (bf16[128,1024]{1,0:T(8,128)(2,1)}, bf16[128,1024]{1,0:T(8,128)(2,1)}, u32[]{:S(2)}, u32[]{:S(2)}) collective-permute-start(bf16[128,1024]{1,0:T(8,128)(2,1)} %bitcast.69), channel_id=1, source_target_pairs={{0,2},{1,3},{2,0},{3,1},{4,6},{5,7},{6,4},{7,5},{8,10},{9,11},{10,... | collective-permute-start | bytes 786440 | tf_op jit(solution)/shard_map/ppermute | solution.py:58
  32.7 3.0 %collective-permute-start.9 = (bf16[64,1024]{1,0:T(8,128)(2,1)}, bf16[64,1024]{1,0:T(8,128)(2,1)}, u32[]{:S(2)}, u32[]{:S(2)}) collective-permute-start(bf16[64,1024]{1,0:T(8,128)(2,1)} %get-tuple-element.12), channel_id=1, source_target_pairs={{0,96},{4,100},{8,104},{12,108},{16,112},{20,116},{24,120},{28,124... | collective-permute-start | bytes 393224 | tf_op jit(solution)/shard_map/ppermute | solution.py:62
  37.3 4.4 %collective-permute-done.9 = bf16[64,1024]{1,0:T(8,128)(2,1)} collective-permute-done((bf16[64,1024]{1,0:T(8,128)(2,1)}, bf16[64,1024]{1,0:T(8,128)(2,1)}, u32[]{:S(2)}, u32[]{:S(2)}) %collective-permute-start.9) | collective-permute-done | bytes 131104 | tf_op jit(solution)/shard_map/ppermute | solution.py:62
  41.7 2.2 %collective-permute-done.8 = bf16[64,1024]{1,0:T(8,128)(2,1)} collective-permute-done((bf16[64,1024]{1,0:T(8,128)(2,1)}, bf16[64,1024]{1,0:T(8,128)(2,1)}, u32[]{:S(2)}, u32[]{:S(2)}) %collective-permute-start.8) | collective-permute-done | bytes 131104 | tf_op jit(solution)/shard_map/ppermute | solution.py:62
  44.0 1.4 %fusion.4 = f32[8,4,8,64]{3,2,1,0:T(8,128)S(1)} fusion(bf16[8,64,3072]{2,1,0:T(8,128)(2,1)S(1)} %bitcast.71, bf16[1,8,8,1024]{3,2,0,1:T(8,128)(2,1)} %bitcast.21, bf16[1,8,8,1024]{3,2,0,1:T(8,128)(2,1)} %bitcast.19, bf16[1,8,8,1024]{3,2,0,1:T(8,128)(2,1)S(1)} %bitcast.92, bf16[1,8,8,1024]{3,2,0,1:T(8,128)(2,1)S(1)} %copy-done.2), kind=kOutput, calls=%fused_computation.13 | convolution fusion | flops 34340864 | bytes 1638400 | tf_op jit(solution)/shard_map/makw,arw->amkr/dot_general | solution.py:116
  46.0 1.8 %collective-permute-start.11 = (f32[128,128]{1,0:T(8,128)S(1)}, f32[128,128]{1,0:T(8,128)S(1)}, u32[]{:S(2)}, u32[]{:S(2)}) collective-permute-start(f32[128,128]{1,0:T(8,128)S(1)} %pad_maximum_fusion.3), channel_id=1, source_target_pairs={{0,2},{1,3},{2,0},{3,1},{4,6},{5,7},{6,4},{7,5},{8,10},{9,11},{10,... | collective-permute-start | bytes 196616 | tf_op jit(solution)/shard_map/ppermute | solution.py:58
  47.8 1.8 %collective-permute-start.10 = (f32[128,128]{1,0:T(8,128)S(1)}, f32[128,128]{1,0:T(8,128)S(1)}, u32[]{:S(2)}, u32[]{:S(2)}) collective-permute-start(f32[128,128]{1,0:T(8,128)S(1)} %pad_maximum_fusion.3), channel_id=1, source_target_pairs={{0,1},{1,0},{2,3},{3,2},{4,5},{5,4},{6,7},{7,6},{8,9},{9,8},{10,11... | collective-permute-start | bytes 196616 | tf_op jit(solution)/shard_map/ppermute | solution.py:58
  49.8 1.2 %collective-permute-done.12 = f32[128,128]{1,0:T(8,128)S(1)} collective-permute-done((f32[128,128]{1,0:T(8,128)S(1)}, f32[128,128]{1,0:T(8,128)S(1)}, u32[]{:S(2)}, u32[]{:S(2)}) %collective-permute-start.12) | collective-permute-done | bytes 65568 | tf_op jit(solution)/shard_map/ppermute | solution.py:58
  51.0 1.0 %collective-permute-start.2 = (bf16[128,1024]{1,0:T(8,128)(2,1)}, bf16[128,1024]{1,0:T(8,128)(2,1)S(1)}, u32[]{:S(2)}, u32[]{:S(2)}) collective-permute-start(bf16[128,1024]{1,0:T(8,128)(2,1)} %bitcast.69), channel_id=1, source_target_pairs={{0,3},{1,2},{2,1},{3,0},{4,7},{5,6},{6,5},{7,4},{8,11},{9,10},{10,... | collective-permute-start | bytes 786440 | tf_op jit(solution)/shard_map/ppermute | solution.py:58
  52.7 2.0 %fusion = bf16[4,8,8,2048]{3,2,0,1:T(8,128)(2,1)S(1)} fusion(bf16[8,4,8,64]{3,2,1,0:T(8,128)(2,1)S(1)} %bitcast.89, bf16[8,64,3072]{2,1,0:T(8,128)(2,1)} %bitcast.72), kind=kOutput, calls=%fused_computation.2 | convolution fusion | flops 67633152 | bytes 3178496 | tf_op jit(solution)/shard_map/amkr,ard->makd/dot_general | solution.py:124
  54.8 2.0 %collective-permute-start.15 = (bf16[64,2048]{1,0:T(8,128)(2,1)S(1)}, bf16[64,2048]{1,0:T(8,128)(2,1)S(1)}, u32[]{:S(2)}, u32[]{:S(2)}) collective-permute-start(bf16[64,2048]{1,0:T(8,128)(2,1)S(1)} %get-tuple-element.8), channel_id=1, source_target_pairs={{0,96},{4,100},{8,104},{12,108},{16,112},{20,116},{24,120},{28,124... | collective-permute-start | bytes 786440 | tf_op jit(solution)/shard_map/ppermute | solution.py:62
  57.5 1.5 %collective-permute-start.13 = (bf16[64,2048]{1,0:T(8,128)(2,1)S(1)}, bf16[64,2048]{1,0:T(8,128)(2,1)S(1)}, u32[]{:S(2)}, u32[]{:S(2)}) collective-permute-start(bf16[64,2048]{1,0:T(8,128)(2,1)S(1)} %get-tuple-element.10), channel_id=1, source_target_pairs={{0,32},{4,36},{8,40},{12,44},{16,48},{20,52},{24,56},{28,60},{32,0... | collective-permute-start | bytes 786440 | tf_op jit(solution)/shard_map/ppermute | solution.py:62
  59.0 1.0 %constant_dynamic-update-slice_fusion.2 = bf16[128,4096]{1,0:T(8,128)(2,1)S(1)} fusion(bf16[128,4096]{1,0:T(8,128)(2,1)S(1)} %constant_dynamic-update-slice_fusion.3, bf16[128,1024]{1,0:T(8,128)(2,1)} %collective-permute-done, s32[]{:T(128)S(6)} %select_n.26), kind=kLoop, calls=%fused_computation.65 | loop fusion | bytes 524292 | tf_op jit(solution)/shard_map/dynamic_update_slice | solution.py:112
  60.0 1.0 %constant_dynamic-update-slice_fusion.1 = bf16[128,4096]{1,0:T(8,128)(2,1)S(1)} fusion(bf16[128,4096]{1,0:T(8,128)(2,1)S(1)} %constant_dynamic-update-slice_fusion.2, bf16[128,1024]{1,0:T(8,128)(2,1)} %collective-permute-done.1, s32[]{:T(128)S(6)} %select_n.27), kind=kLoop, calls=%fused_computation.64 | loop fusion | bytes 524292 | tf_op jit(solution)/shard_map/dynamic_update_slice | solution.py:112
  61.0 5.8 %collective-permute-done.15 = bf16[64,2048]{1,0:T(8,128)(2,1)S(1)} collective-permute-done((bf16[64,2048]{1,0:T(8,128)(2,1)S(1)}, bf16[64,2048]{1,0:T(8,128)(2,1)S(1)}, u32[]{:S(2)}, u32[]{:S(2)}) %collective-permute-start.15) | collective-permute-done | bytes 262176 | tf_op jit(solution)/shard_map/ppermute | solution.py:62
  68.1 9.0 %fusion.1 = bf16[128,2048]{1,0:T(8,128)(2,1)} fusion(f32[128,2048]{1,0:T(8,128)S(1)} %fusion.5, bf16[128,4096]{1,0:T(8,128)(2,1)S(1)} %constant_dynamic-update-slice_fusion, bf16[4096,2048]{1,0:T(8,128)(2,1)} %param.17), kind=kOutput, calls=%fused_computation.4 | convolution fusion | flops 2148007936 | bytes 19398656 | tf_op jit(solution)/shard_map/dot_general | solution.py:113
  (59 shorter events, 10.4 us)
Async XLA Ops:
  0.0 8.0 %copy-start = (bf16[128,128]{1,0:T(8,128)(2,1)S(1)}, bf16[128,128]{1,0:T(8,128)(2,1)}, u32[]{:S(2)}) copy-start(bf16[128,128]{1,0:T(8,128)(2,1)} %param.12) | copy-start | bytes 98308
  1.1 21.7 %collective-permute-start.5 = (bf16[64,3072]{1,0:T(8,128)(2,1)S(1)}, bf16[64,3072]{1,0:T(8,128)(2,1)S(1)}, u32[]{:S(2)}, u32[]{:S(2)}) collective-permute-start(bf16[64,3072]{1,0:T(8,128)(2,1)S(1)} %get-tuple-element.16), channel_id=1, source_target_pairs={{0,24},{4,28},{8,16},{12,20},{16,8},{20,12},{24,0},{28,4},{32,56},... | collective-permute-start | bytes 1179656 | tf_op jit(solution)/shard_map/ppermute | solution.py:62
  5.3 17.5 %collective-permute-start.4 = (bf16[64,3072]{1,0:T(8,128)(2,1)S(1)}, bf16[64,3072]{1,0:T(8,128)(2,1)S(1)}, u32[]{:S(2)}, u32[]{:S(2)}) collective-permute-start(bf16[64,3072]{1,0:T(8,128)(2,1)S(1)} %get-tuple-element.16), channel_id=1, source_target_pairs={{0,16},{4,20},{8,24},{12,28},{16,0},{20,4},{24,8},{28,12},{32,48},... | collective-permute-start | bytes 1179656 | tf_op jit(solution)/shard_map/ppermute | solution.py:62
  5.3 18.2 %collective-permute-start.3 = (bf16[64,3072]{1,0:T(8,128)(2,1)S(1)}, bf16[64,3072]{1,0:T(8,128)(2,1)S(1)}, u32[]{:S(2)}, u32[]{:S(2)}) collective-permute-start(bf16[64,3072]{1,0:T(8,128)(2,1)S(1)} %get-tuple-element.16), channel_id=1, source_target_pairs={{0,8},{4,12},{8,0},{12,4},{16,24},{20,28},{24,16},{28,20},{32,40},... | collective-permute-start | bytes 1179656 | tf_op jit(solution)/shard_map/ppermute | solution.py:62
  8.0 17.0 %slice-start = ((s8[8388608]{0:T(1024)(128)(4,1)}), s8[4194304]{0:T(1024)(128)(4,1)S(1)}, s32[]{:S(2)}) async-start(s8[8388608]{0:T(1024)(128)(4,1)} %bitcast.90), calls=%async_computation | async-start | bytes 8388608
  8.3 16.7 %slice-start.1 = ((s8[8388608]{0:T(1024)(128)(4,1)}), s8[4194304]{0:T(1024)(128)(4,1)S(1)}, s32[]{:S(2)}) async-start(s8[8388608]{0:T(1024)(128)(4,1)} %bitcast.90), calls=%async_computation.1 | async-start | bytes 8388608
  23.5 1.5 %copy-start.3 = (bf16[128,128]{1,0:T(8,128)(2,1)S(1)}, bf16[128,128]{1,0:T(8,128)(2,1)}, u32[]{:S(2)}) copy-start(bf16[128,128]{1,0:T(8,128)(2,1)} %param.13) | copy-start | bytes 98308
  24.9 11.4 %collective-permute-start.6 = (bf16[4,64,3072]{2,1,0:T(8,128)(2,1)}, bf16[4,64,3072]{2,1,0:T(8,128)(2,1)S(1)}, u32[]{:S(2)}, u32[]{:S(2)}) collective-permute-start(bf16[4,64,3072]{2,1,0:T(8,128)(2,1)} %get-tuple-element.6), channel_id=1, source_target_pairs={{0,4},{4,0},{8,12},{12,8},{16,20},{20,16},{24,28},{28,24},{32,36},... | collective-permute-start | bytes 4718600 | tf_op jit(solution)/shard_map/ppermute | solution.py:62
  25.0 6.3 %copy-start.4 = (s32[32]{0:T(128)S(1)}, s32[32]{0:T(128)}, u32[]{:S(2)}) copy-start(s32[32]{0:T(128)} %param.19) | copy-start | bytes 388
  25.0 6.3 %copy-start.5 = (s32[128]{0:T(128)S(1)}, s32[128]{0:T(128)}, u32[]{:S(2)}) copy-start(s32[128]{0:T(128)} %param.18) | copy-start | bytes 1540
  27.1 30.3 %collective-permute-start = (bf16[128,1024]{1,0:T(8,128)(2,1)}, bf16[128,1024]{1,0:T(8,128)(2,1)}, u32[]{:S(2)}, u32[]{:S(2)}) collective-permute-start(bf16[128,1024]{1,0:T(8,128)(2,1)} %bitcast.69), channel_id=1, source_target_pairs={{0,1},{1,0},{2,3},{3,2},{4,5},{5,4},{6,7},{7,6},{8,9},{9,8},{10,11... | collective-permute-start | bytes 786440 | tf_op jit(solution)/shard_map/ppermute | solution.py:58
  28.6 31.3 %collective-permute-start.1 = (bf16[128,1024]{1,0:T(8,128)(2,1)}, bf16[128,1024]{1,0:T(8,128)(2,1)}, u32[]{:S(2)}, u32[]{:S(2)}) collective-permute-start(bf16[128,1024]{1,0:T(8,128)(2,1)} %bitcast.69), channel_id=1, source_target_pairs={{0,2},{1,3},{2,0},{3,1},{4,6},{5,7},{6,4},{7,5},{8,10},{9,11},{10,... | collective-permute-start | bytes 786440 | tf_op jit(solution)/shard_map/ppermute | solution.py:58
  32.7 9.0 %collective-permute-start.9 = (bf16[64,1024]{1,0:T(8,128)(2,1)}, bf16[64,1024]{1,0:T(8,128)(2,1)}, u32[]{:S(2)}, u32[]{:S(2)}) collective-permute-start(bf16[64,1024]{1,0:T(8,128)(2,1)} %get-tuple-element.12), channel_id=1, source_target_pairs={{0,96},{4,100},{8,104},{12,108},{16,112},{20,116},{24,120},{28,124... | collective-permute-start | bytes 393224 | tf_op jit(solution)/shard_map/ppermute | solution.py:62
  35.7 8.2 %collective-permute-start.8 = (bf16[64,1024]{1,0:T(8,128)(2,1)}, bf16[64,1024]{1,0:T(8,128)(2,1)}, u32[]{:S(2)}, u32[]{:S(2)}) collective-permute-start(bf16[64,1024]{1,0:T(8,128)(2,1)} %get-tuple-element.13), channel_id=1, source_target_pairs={{0,64},{4,68},{8,72},{12,76},{16,80},{20,84},{24,88},{28,92},{32,9... | collective-permute-start | bytes 393224 | tf_op jit(solution)/shard_map/ppermute | solution.py:62
  36.4 7.6 %collective-permute-start.7 = (bf16[64,1024]{1,0:T(8,128)(2,1)}, bf16[64,1024]{1,0:T(8,128)(2,1)S(1)}, u32[]{:S(2)}, u32[]{:S(2)}) collective-permute-start(bf16[64,1024]{1,0:T(8,128)(2,1)} %get-tuple-element.14), channel_id=1, source_target_pairs={{0,32},{4,36},{8,40},{12,44},{16,48},{20,52},{24,56},{28,60},{32,0... | collective-permute-start | bytes 393224 | tf_op jit(solution)/shard_map/ppermute | solution.py:62
  37.1 6.9 %copy-start.2 = (bf16[1,8,8,1024]{3,2,0,1:T(8,128)(2,1)S(1)}, bf16[1,8,8,1024]{3,2,0,1:T(8,128)(2,1)}, u32[]{:S(2)}) copy-start(bf16[1,8,8,1024]{3,2,0,1:T(8,128)(2,1)} %get-tuple-element.11) | copy-start | bytes 393220
  37.3 12.4 %copy-start.1 = (bf16[4,2,64,3072]{3,2,1,0:T(8,128)(2,1)}, bf16[4,2,64,3072]{3,2,1,0:T(8,128)(2,1)S(1)}, u32[]{:S(2)}) copy-start(bf16[4,2,64,3072]{3,2,1,0:T(8,128)(2,1)S(1)} %copy.17) | copy-start | bytes 9437188
  45.5 5.6 %collective-permute-start.12 = (f32[128,128]{1,0:T(8,128)S(1)}, f32[128,128]{1,0:T(8,128)S(1)}, u32[]{:S(2)}, u32[]{:S(2)}) collective-permute-start(f32[128,128]{1,0:T(8,128)S(1)} %pad_maximum_fusion.3), channel_id=1, source_target_pairs={{0,3},{1,2},{2,1},{3,0},{4,7},{5,6},{6,5},{7,4},{8,11},{9,10},{10,... | collective-permute-start | bytes 196616 | tf_op jit(solution)/shard_map/ppermute | solution.py:58
  46.0 6.0 %collective-permute-start.11 = (f32[128,128]{1,0:T(8,128)S(1)}, f32[128,128]{1,0:T(8,128)S(1)}, u32[]{:S(2)}, u32[]{:S(2)}) collective-permute-start(f32[128,128]{1,0:T(8,128)S(1)} %pad_maximum_fusion.3), channel_id=1, source_target_pairs={{0,2},{1,3},{2,0},{3,1},{4,6},{5,7},{6,4},{7,5},{8,10},{9,11},{10,... | collective-permute-start | bytes 196616 | tf_op jit(solution)/shard_map/ppermute | solution.py:58
  47.8 4.8 %collective-permute-start.10 = (f32[128,128]{1,0:T(8,128)S(1)}, f32[128,128]{1,0:T(8,128)S(1)}, u32[]{:S(2)}, u32[]{:S(2)}) collective-permute-start(f32[128,128]{1,0:T(8,128)S(1)} %pad_maximum_fusion.3), channel_id=1, source_target_pairs={{0,1},{1,0},{2,3},{3,2},{4,5},{5,4},{6,7},{7,6},{8,9},{9,8},{10,11... | collective-permute-start | bytes 196616 | tf_op jit(solution)/shard_map/ppermute | solution.py:58
  51.0 9.9 %collective-permute-start.2 = (bf16[128,1024]{1,0:T(8,128)(2,1)}, bf16[128,1024]{1,0:T(8,128)(2,1)S(1)}, u32[]{:S(2)}, u32[]{:S(2)}) collective-permute-start(bf16[128,1024]{1,0:T(8,128)(2,1)} %bitcast.69), channel_id=1, source_target_pairs={{0,3},{1,2},{2,1},{3,0},{4,7},{5,6},{6,5},{7,4},{8,11},{9,10},{10,... | collective-permute-start | bytes 786440 | tf_op jit(solution)/shard_map/ppermute | solution.py:58
  54.8 12.0 %collective-permute-start.15 = (bf16[64,2048]{1,0:T(8,128)(2,1)S(1)}, bf16[64,2048]{1,0:T(8,128)(2,1)S(1)}, u32[]{:S(2)}, u32[]{:S(2)}) collective-permute-start(bf16[64,2048]{1,0:T(8,128)(2,1)S(1)} %get-tuple-element.8), channel_id=1, source_target_pairs={{0,96},{4,100},{8,104},{12,108},{16,112},{20,116},{24,120},{28,124... | collective-permute-start | bytes 786440 | tf_op jit(solution)/shard_map/ppermute | solution.py:62
  56.8 10.4 %collective-permute-start.14 = (bf16[64,2048]{1,0:T(8,128)(2,1)S(1)}, bf16[64,2048]{1,0:T(8,128)(2,1)S(1)}, u32[]{:S(2)}, u32[]{:S(2)}) collective-permute-start(bf16[64,2048]{1,0:T(8,128)(2,1)S(1)} %get-tuple-element.9), channel_id=1, source_target_pairs={{0,64},{4,68},{8,72},{12,76},{16,80},{20,84},{24,88},{28,92},{32,9... | collective-permute-start | bytes 786440 | tf_op jit(solution)/shard_map/ppermute | solution.py:62
  57.5 10.3 %collective-permute-start.13 = (bf16[64,2048]{1,0:T(8,128)(2,1)S(1)}, bf16[64,2048]{1,0:T(8,128)(2,1)S(1)}, u32[]{:S(2)}, u32[]{:S(2)}) collective-permute-start(bf16[64,2048]{1,0:T(8,128)(2,1)S(1)} %get-tuple-element.10), channel_id=1, source_target_pairs={{0,32},{4,36},{8,40},{12,44},{16,48},{20,52},{24,56},{28,60},{32,0... | collective-permute-start | bytes 786440 | tf_op jit(solution)/shard_map/ppermute | solution.py:62

commit v2 on v1

v2 whole, which is shorter than its diff:
```python
import functools
import math

import jax
import jax.numpy as jnp
from jax import lax
from jax.experimental import pallas as pl
from jax.experimental.pallas import tpu as pltpu
from jax.sharding import PartitionSpec as P

HEADS = 32
KV_HEADS = 4
HEAD_DIM = 128
CAP = 8
Z_CHIPS = 4
CORES = 2
RING = 4
GROUP = HEADS // KV_HEADS
BLOCK = 32
ATTEND_VMEM = 63 * 2**20
STAGED = 6
DEPTH = 512


def slot_positions(request_adapter, table_ref):
    i32, f32 = jnp.int32, jnp.float32
    requests = request_adapter.shape[1]
    slot = jnp.zeros_like(request_adapter)
    for adapter in range(table_ref.shape[0]):
        slot = jnp.where(request_adapter == adapter, table_ref[adapter], slot)
    square = (requests, requests)
    across = jnp.broadcast_to(slot.astype(f32), square)
    earlier = (across.T == across) & (
        lax.broadcasted_iota(i32, square, 0) < lax.broadcasted_iota(i32, square, 1)
    )
    count = jnp.sum(jnp.where(earlier, 1.0, 0.0), axis=0, keepdims=True).astype(i32)
    return (slot ^ lax.axis_index("dp")) * CAP + count


def attend_kernel(*refs):
    sources, (key_hbm, value_hbm), refs = refs[:STAGED], refs[STAGED : STAGED + 2], refs[STAGED + 2 :]
    attended_ref, bucket_refs, refs = refs[0], refs[1 : 1 + RING], refs[1 + RING :]
    staged, refs = refs[:STAGED], refs[STAGED:]
    length_ref, table_ref, adapter_ref, query_ref, token_key_ref, token_value_ref = staged
    key_ref, value_ref, heads_ref, fresh_key_ref, fresh_value_ref, mixed_ref, used_ref = refs[:7]
    staged_sem, key_sem, value_sem = refs[7:]
    f32, bf16 = jnp.float32, jnp.bfloat16
    requests, positions, _ = key_ref.shape
    score_scale = 1.0 / math.sqrt(HEAD_DIM)

    def fetch(source, target, sem, c):
        at = pl.ds(c * BLOCK, BLOCK)
        return pltpu.make_async_copy(source.at[at], target.at[at], sem.at[c])

    staging = [
        pltpu.make_async_copy(source, target, staged_sem.at[i])
        for i, (source, target) in enumerate(zip(sources, staged))
    ]
    for copy in staging:
        copy.start()
    for c in range(requests // BLOCK):
        fetch(key_hbm, key_ref, key_sem, c).start()
        fetch(value_hbm, value_ref, value_sem, c).start()
    for copy in staging:
        copy.wait()
    slots_at = slot_positions(adapter_ref[...], table_ref)

    for c in range(requests // BLOCK):
        rows = slice(c * BLOCK, (c + 1) * BLOCK)
        fresh_keys = token_key_ref[rows, :].astype(f32)
        fresh_values = token_value_ref[rows, :].astype(f32)
        for h in range(GROUP):
            at = pl.ds(h, BLOCK, stride=GROUP)
            heads_ref[at, :] = query_ref[rows, h * HEAD_DIM : (h + 1) * HEAD_DIM].astype(f32)
            fresh_key_ref[at, :] = fresh_keys
            fresh_value_ref[at, :] = fresh_values
        for r in range(BLOCK):
            used_ref[r * GROUP : (r + 1) * GROUP, :] = jnp.full(
                (GROUP, positions), length_ref[c * BLOCK + r], jnp.int32
            )
        heads = heads_ref[...]
        fetch(key_hbm, key_ref, key_sem, c).wait()
        score = lax.dot_general(
            heads.reshape(BLOCK, GROUP, HEAD_DIM).astype(bf16),
            key_ref[rows],
            (((2,), (2,)), ((0,), (0,))),
            preferred_element_type=f32,
        )
        score = score.reshape(BLOCK * GROUP, positions) * score_scale
        fresh = jnp.sum(heads * fresh_key_ref[...], axis=1, keepdims=True) * score_scale
        place = lax.broadcasted_iota(jnp.int32, score.shape, 1)
        score = jnp.where(place < used_ref[...], score, -jnp.inf)
        row_max = jnp.maximum(jnp.max(score, axis=1, keepdims=True), fresh)
        weight = jnp.exp(score - row_max)
        fresh_weight = jnp.exp(fresh - row_max)
        weight_sum = jnp.sum(weight, axis=1, keepdims=True) + fresh_weight
        fetch(value_hbm, value_ref, value_sem, c).wait()
        mixed = lax.dot_general(
            weight.reshape(BLOCK, GROUP, positions).astype(bf16),
            value_ref[rows],
            (((2,), (1,)), ((0,), (0,))),
            preferred_element_type=f32,
        ).reshape(BLOCK * GROUP, HEAD_DIM)
        mixed = mixed + fresh_weight.astype(bf16).astype(f32) * fresh_value_ref[...]
        mixed_ref[...] = mixed / weight_sum
        for h in range(GROUP):
            attended_ref[0, rows, h * HEAD_DIM : (h + 1) * HEAD_DIM] = mixed_ref[
                pl.ds(h, BLOCK, stride=GROUP), :
            ].astype(bf16)

    attended = attended_ref[0]
    for k in range(1, RING):
        attended_ref[k] = attended
    for m, bucket_ref in enumerate(bucket_refs):
        slots = bucket_ref.shape[0]
        wanted = m * slots + lax.broadcasted_iota(jnp.int32, (slots, requests), 0)
        placing = jnp.where(wanted == slots_at, 1.0, 0.0).astype(bf16)
        bucket_ref[...] = jnp.dot(placing, attended, preferred_element_type=f32).astype(bf16)


def attend(
    queries,
    token_keys,
    token_values,
    cached_key_rows,
    cached_value_rows,
    cache_length,
    request_adapter,
    adapter_table_row,
    slots,
):
    requests, features = queries.shape
    positions = cached_key_rows.shape[1]
    vmem = pl.BlockSpec(memory_space=pltpu.VMEM)
    hbm = pl.BlockSpec(memory_space=pltpu.HBM)
    per_head = pltpu.VMEM((BLOCK * GROUP, HEAD_DIM), jnp.float32)
    fetches = pltpu.SemaphoreType.DMA((requests // BLOCK,))
    return pl.pallas_call(
        attend_kernel,
        in_specs=[hbm] * (STAGED + 2),
        out_specs=[vmem] * (1 + RING),
        out_shape=[jax.ShapeDtypeStruct((RING, requests, features), jnp.bfloat16)]
        + [jax.ShapeDtypeStruct((slots, features), jnp.bfloat16)] * RING,
        scratch_shapes=[
            pltpu.SMEM(cache_length.shape, jnp.int32),
            pltpu.SMEM(adapter_table_row.shape, jnp.int32),
            pltpu.VMEM((1, requests), jnp.int32),
            pltpu.VMEM(queries.shape, jnp.bfloat16),
            pltpu.VMEM(token_keys.shape, jnp.bfloat16),
            pltpu.VMEM(token_values.shape, jnp.bfloat16),
        ]
        + [pltpu.VMEM(cached_key_rows.shape, jnp.bfloat16)] * 2
        + [per_head] * 4
        + [pltpu.VMEM((BLOCK * GROUP, positions), jnp.int32)]
        + [pltpu.SemaphoreType.DMA((STAGED,)), fetches, fetches],
        compiler_params=pltpu.CompilerParams(vmem_limit_bytes=ATTEND_VMEM),
        cost_estimate=pl.CostEstimate(
            flops=4 * requests * GROUP * positions * HEAD_DIM,
            bytes_accessed=4 * requests * positions * HEAD_DIM,
            transcendentals=requests * GROUP * positions,
        ),
    )(
        cache_length,
        adapter_table_row,
        request_adapter.reshape(1, requests),
        queries,
        token_keys,
        token_values,
        cached_key_rows,
        cached_value_rows,
    )


def down_kernel(*refs):
    routed, weights, out_ref = refs[:RING], refs[RING:-1], refs[-1]
    rank = weights[0].shape[0]
    features = routed[0].shape[1]
    pair = CORES * CAP
    for k in range(Z_CHIPS):
        rows = jnp.concatenate([r[k * pair : (k + 1) * pair, :] for r in routed], axis=0)
        products = [
            lax.dot_general(
                rows,
                w[:, :features],
                (((1,), (1,)), ((), ())),
                preferred_element_type=jnp.float32,
            )
            for w in weights[k * CORES : (k + 1) * CORES]
        ]
        for m in range(RING):
            at = (k * RING + m) * CAP
            for j, product in enumerate(products):
                row = m * pair + j * CAP
                out_ref[at : at + CAP, j * rank : (j + 1) * rank] = product[row : row + CAP, :]


def down(routed, weights):
    rank = weights[0].shape[0]
    vmem = pl.BlockSpec(memory_space=pltpu.VMEM)
    return pl.pallas_call(
        down_kernel,
        in_specs=[vmem] * (len(routed) + len(weights)),
        out_specs=vmem,
        out_shape=jax.ShapeDtypeStruct((Z_CHIPS * RING * CAP, CORES * rank), jnp.float32),
        compiler_params=pltpu.CompilerParams(vmem_limit_bytes=16 * 2**20),
    )(*routed, *weights)


def up_kernel(columns, *refs):
    partials, weights, deltas = refs[:RING], refs[RING:-RING], refs[-RING:]
    rank = weights[0].shape[0]
    pair = CORES * CAP
    total = partials[0][...] + partials[1][...] + partials[2][...] + partials[3][...]
    for k in range(Z_CHIPS):
        part = total[k * RING * CAP : (k + 1) * RING * CAP, :]
        spread = []
        for m in range(RING):
            spread += [part[m * CAP : (m + 1) * CAP, :]] * CORES
        spread = jnp.concatenate(spread, axis=0)
        row = lax.broadcasted_iota(jnp.int32, spread.shape, 0)
        lane = lax.broadcasted_iota(jnp.int32, spread.shape, 1)
        low_rank = jnp.where((row // CAP) % CORES == lane // rank, spread, 0.0)
        low_rank = low_rank.astype(jnp.bfloat16)
        delta = 0.0
        for j, w in enumerate(weights[k * CORES : (k + 1) * CORES]):
            delta += jnp.dot(
                low_rank[:, j * rank : (j + 1) * rank],
                w[:, w.shape[1] - columns :],
                preferred_element_type=jnp.float32,
            )
        delta = delta.astype(jnp.bfloat16)
        for m, delta_ref in enumerate(deltas):
            delta_ref[k * pair : (k + 1) * pair, :] = delta[m * pair : (m + 1) * pair, :]


def up(partials, weights, columns):
    rows = Z_CHIPS * CORES * CAP
    vmem = pl.BlockSpec(memory_space=pltpu.VMEM)
    return pl.pallas_call(
        functools.partial(up_kernel, columns),
        in_specs=[vmem] * (len(partials) + len(weights)),
        out_specs=[vmem] * RING,
        out_shape=[jax.ShapeDtypeStruct((rows, columns), jnp.bfloat16)] * RING,
        compiler_params=pltpu.CompilerParams(vmem_limit_bytes=16 * 2**20),
    )(*partials, *weights)


def project_kernel(piece_hbm, weight_hbm, out_ref, piece_ref, weight_ref, piece_sem, sem):
    depth = weight_ref.shape[0] // sem.shape[0]
    per_piece = piece_ref.shape[2] // depth

    def fetch(c):
        at = pl.ds(c * depth, depth)
        return pltpu.make_async_copy(weight_hbm.at[at], weight_ref.at[at], sem.at[c])

    pieces = pltpu.make_async_copy(piece_hbm, piece_ref, piece_sem)
    pieces.start()
    for c in range(sem.shape[0]):
        fetch(c).start()
    pieces.wait()
    for c in range(sem.shape[0]):
        fetch(c).wait()
        piece, part = c // per_piece, c % per_piece
        product = jnp.dot(
            piece_ref[piece, :, part * depth : (part + 1) * depth],
            weight_ref[c * depth : (c + 1) * depth, :],
            preferred_element_type=jnp.float32,
        )
        if c == 0:
            out_ref[...] = product
        else:
            out_ref[...] += product


def project(pieces, weights):
    count, requests, features = pieces.shape
    columns = weights.shape[1]
    hbm = pl.BlockSpec(memory_space=pltpu.HBM)
    return pl.pallas_call(
        project_kernel,
        in_specs=[hbm, hbm],
        out_specs=pl.BlockSpec(memory_space=pltpu.VMEM),
        out_shape=jax.ShapeDtypeStruct((requests, columns), jnp.float32),
        scratch_shapes=[
            pltpu.VMEM(pieces.shape, jnp.bfloat16),
            pltpu.VMEM(weights.shape, jnp.bfloat16),
            pltpu.SemaphoreType.DMA,
            pltpu.SemaphoreType.DMA((weights.shape[0] // DEPTH,)),
        ],
        compiler_params=pltpu.CompilerParams(vmem_limit_bytes=52 * 2**20),
        cost_estimate=pl.CostEstimate(
            flops=2 * count * requests * features * columns,
            bytes_accessed=2 * count * features * columns,
            transcendentals=0,
        ),
    )(pieces, weights)


def swap_tensor(value, k):
    return lax.ppermute(value, "tensor", [(i, i ^ k) for i in range(RING)])


def swap_dp(value, k):
    return lax.ppermute(value, "dp", [(i, i ^ k) for i in range(RING * Z_CHIPS * CORES)])


def swap_y(value, k):
    return swap_dp(value, k * Z_CHIPS * CORES)


def swap_z(value, k):
    return swap_dp(value, k * CORES)


def swap_core(value):
    return swap_dp(value, 1)


def on_device(
    queries,
    token_keys,
    token_values,
    cached_key_rows,
    cached_value_rows,
    cache_length,
    output_projection,
    request_adapter,
    adapter_table_row,
    adapter_down_weight,
    adapter_up_weight,
):
    bf16, f32 = jnp.bfloat16, jnp.float32
    requests = queries.shape[0]
    columns = output_projection.shape[1]
    owned = Z_CHIPS * CORES
    here = lax.axis_index("dp")

    down_here, up_here = adapter_down_weight[0], adapter_up_weight[0]
    both = jnp.concatenate([down_here, up_here], axis=1)
    over_z = [swap_z(both, k) for k in range(1, Z_CHIPS)]
    both_other = swap_core(both)

    attended, *placed = attend(
        queries,
        token_keys,
        token_values,
        cached_key_rows,
        cached_value_rows,
        cache_length,
        request_adapter,
        adapter_table_row,
        owned * CAP,
    )
    pieces = lax.all_to_all(attended, "tensor", 0, 0)
    placed, over_z, both_other, request_adapter = lax.optimization_barrier(
        (placed, over_z, both_other, request_adapter)
    )
    routed = [placed[0]] + [swap_y(placed[m], m) for m in range(1, RING)]
    table = [both, both_other]
    for w in over_z:
        table += [w, swap_core(w)]

    every_adapter = adapter_table_row.shape[0]
    matches = request_adapter[:, None] == jnp.arange(every_adapter, dtype=jnp.int32)[None, :]
    slot_of = jnp.sum(jnp.where(matches, adapter_table_row[None, :], 0), axis=1)
    order = jnp.arange(requests, dtype=jnp.int32)
    earlier = (slot_of[:, None] == slot_of[None, :]) & (order[:, None] > order[None, :])
    position = (slot_of ^ here) * CAP + jnp.sum(earlier.astype(jnp.int32), axis=1)
    placing = (
        position[:, None] == jnp.arange(every_adapter * CAP, dtype=jnp.int32)[None, :]
    ).astype(bf16)

    partial = down(routed, table)
    partials = [partial] + [swap_tensor(partial, k) for k in range(1, RING)]
    partials, pieces = lax.optimization_barrier((partials, pieces))
    projected = project(pieces, output_projection)

    delta = up(partials, table, columns)
    back = [delta[0]] + [swap_y(delta[m], m) for m in range(1, RING)]
    returned = jnp.dot(placing, jnp.concatenate(back, axis=0), preferred_element_type=f32)
    return (projected + returned).astype(bf16)


def solution(mesh):
    in_specs = (
        P("dp", "tensor"),
        P("dp", "tensor"),
        P("dp", "tensor"),
        P("dp", None, "tensor"),
        P("dp", None, "tensor"),
        P("dp"),
        P(None, "tensor"),
        P("dp"),
        P(),
        P("dp", None, "tensor"),
        P("dp", None, "tensor"),
    )
    out_specs = P("dp", "tensor")
    return jax.shard_map(
        on_device, mesh=mesh, in_specs=in_specs, out_specs=out_specs, check_vma=False
    )
```

time: 77.4 us -> 67.4 us (0.87)
  Pallas kernels: 0 us -> 23.4 us
  matrix products: 20.4 us -> 0.35 us
  waiting for transfers between devices: 24.1 us -> 14.5 us
  local copies, waits for them, and re-layouts: 5.07 us -> 0.03 us
  starting transfers between devices: 22.8 us -> 26.6 us
  other arithmetic: 4.32 us -> 2.17 us
    pallas_call x0 -> x4, Pallas kernels: none -> 23.4 us  [the longest x1 11.3 us: attend(): pl.pallas_call(attend_kernel, in_specs=[hbm] * (STAGED + 2), out_specs=[v...]
    dot_general x8 -> x1, matrix products: 20.4 us -> 0.35 us  [on_device(): jnp.dot(placing, jnp.concatenate(back, axis=0), preferred_element_type=f32)]
    ppermute x10 -> x13, waiting for transfers between devices: 22.3 us -> 10.1 us  [swap_dp(): lax.ppermute(value, 'dp', [(i, i ^ k) for i in range(RING * Z_CHIPS * COR...]
    ppermute x6 -> x3, starting transfers between devices: 9.38 us -> 4.12 us  [swap_tensor(): return lax.ppermute(value, 'tensor', [(i, i ^ k) for i in range(RING)])]
    ppermute x10 -> x13, starting transfers between devices: 13.4 us -> 18 us  [swap_dp(): lax.ppermute(value, 'dp', [(i, i ^ k) for i in range(RING * Z_CHIPS * COR...]
    all_to_all x0 -> x1, starting transfers between devices: none -> 4.44 us  [on_device(): pieces = lax.all_to_all(attended, 'tensor', 0, 0)]
    another operation x6 -> x0, other arithmetic: 2.81 us -> none  [the longest x2 1.71 us: on_device(): jnp.stack([over_z, swap_dp(over_z, 1)], axis=1)]
    ppermute x6 -> x3, waiting for transfers between devices: 1.79 us -> 4.42 us  [swap_tensor(): return lax.ppermute(value, 'tensor', [(i, i ^ k) for i in range(RING)])]
  transfers between devices with their start and end apart: 16 -> 17, of which waited for: 9 -> 8; matrix products, arithmetic and copies ran while one was open for 23% -> 0% of each run, Pallas kernels for 0% -> 32%
where the time goes in v2:
time: 67.4 us; the launch traced here: 67.1 us
  starting transfers between devices  26.6 us (39%)
  Pallas kernels  23.4 us (35%)
  waiting for transfers between devices  14.5 us (22%)
  other arithmetic  2.17 us (3%)
    ppermute x13, starting transfers between devices, swap_dp(): lax.ppermute(value, 'dp', [(i, i ^ k) for i in range(RING * Z_CHIPS * COR...  18 us
    pallas_call x1, Pallas kernels, attend(): pl.pallas_call(attend_kernel, in_specs=[hbm] * (STAGED + 2), out_specs=[v...  11.3 us
    ppermute x13, waiting for transfers between devices, swap_dp(): lax.ppermute(value, 'dp', [(i, i ^ k) for i in range(RING * Z_CHIPS * COR...  10.1 us
    pallas_call x1, Pallas kernels, project(): pl.pallas_call(project_kernel, in_specs=[hbm, hbm], out_specs=pl.BlockSpe...  8.36 us
    all_to_all x1, starting transfers between devices, on_device(): pieces = lax.all_to_all(attended, 'tensor', 0, 0)  4.44 us
    ppermute x3, waiting for transfers between devices, swap_tensor(): return lax.ppermute(value, 'tensor', [(i, i ^ k) for i in range(RING)])  4.42 us
    ppermute x3, starting transfers between devices, swap_tensor(): return lax.ppermute(value, 'tensor', [(i, i ^ k) for i in range(RING)])  4.12 us
    pallas_call x1, Pallas kernels, up(): pl.pallas_call(functools.partial(up_kernel, columns), in_specs=[vmem] * (...  1.99 us
  transfers between devices with their start and end apart: 17, of which 8 were waited for; matrix products, arithmetic and copies ran while one was open for 0% of the time, Pallas kernels for 32%

profile of v2, /device:TPU:0, one launch (start us, length us, event | category | flops | bytes accessed | tf_op | source)
XLA Modules:
  0.0 67.1 jit_solution(4068584704243309266)
XLA Ops:
  0.0 1.0 %pad_maximum_fusion.refs_4_ = bf16[64,3072]{1,0:T(8,128)(2,1)S(1)} fusion(bf16[64,2048]{1,0:T(8,128)(2,1)} %bitcast.3, bf16[64,1024]{1,0:T(8,128)(2,1)} %bitcast.4), kind=kLoop, calls=%fused_computation.9 | loop fusion | flops 786432 | bytes 786432 | tf_op jit(solution)/shard_map/concatenate | solution.py:339
  1.1 4.2 %collective-permute-start.2 = (bf16[64,3072]{1,0:T(8,128)(2,1)S(1)}, bf16[64,3072]{1,0:T(8,128)(2,1)}, u32[]{:S(2)}, u32[]{:S(2)}) collective-permute-start(bf16[64,3072]{1,0:T(8,128)(2,1)S(1)} %pad_maximum_fusion.refs_4_), channel_id=1, source_target_pairs={{0,24},{4,28},{8,16},{12,20},{16,8},{20,12},{24,0},{28,4},{32,56},... | collective-permute-start | bytes 1179656 | tf_op jit(solution)/shard_map/ppermute | solution.py:304
  5.3 0.9 %collective-permute-start = (bf16[64,3072]{1,0:T(8,128)(2,1)S(1)}, bf16[64,3072]{1,0:T(8,128)(2,1)}, u32[]{:S(2)}, u32[]{:S(2)}) collective-permute-start(bf16[64,3072]{1,0:T(8,128)(2,1)S(1)} %pad_maximum_fusion.refs_4_), channel_id=1, source_target_pairs={{0,8},{4,12},{8,0},{12,4},{16,24},{20,28},{24,16},{28,20},{32,40},... | collective-permute-start | bytes 1179656 | tf_op jit(solution)/shard_map/ppermute | solution.py:304
  6.3 11.3 %shard_map.109 = (bf16[4,128,1024]{2,1,0:T(8,128)(2,1)}, bf16[64,1024]{1,0:T(8,128)(2,1)}, bf16[64,1024]{1,0:T(8,128)(2,1)}, bf16[64,1024]{1,0:T(8,128)(2,1)}, bf16[64,1024]{1,0:T(8,128)(2,1)}) custom-call(s32[128]{0:T(128)} %refs_0_.1, s32[32]{0:T(128)} %refs_1_.1, s32[1,128]{1,0:T(1,128)} %bitcast.5, bf16[128,1024]{1,0:T(8,128)(2,1)} %refs_3_.1, ...), custom_call_target="tpu_custom_call" | custom-call | flops 134217728 | bytes 16777216 | tf_op jit(solution)/shard_map/pallas_call | solution.py:138
  17.6 4.4 %all-to-all-start = ((bf16[4,128,1024]{2,1,0:T(8,128)(2,1)}), bf16[4,128,1024]{2,1,0:T(8,128)(2,1)}, u32[]{:S(2)}, u32[]{:S(2)}) async-start(bf16[4,128,1024]{2,1,0:T(8,128)(2,1)} %get-tuple-element.40), calls=%async_computation | async-start | bytes 2097152 | tf_op jit(solution)/shard_map/all_to_all | solution.py:354
  22.1 1.5 %collective-permute-done.2.refs_10_ = bf16[64,3072]{1,0:T(8,128)(2,1)} collective-permute-done((bf16[64,3072]{1,0:T(8,128)(2,1)S(1)}, bf16[64,3072]{1,0:T(8,128)(2,1)}, u32[]{:S(2)}, u32[]{:S(2)}) %collective-permute-start.2) | collective-permute-done | bytes 393248 | tf_op jit(solution)/shard_map/ppermute | solution.py:304
  23.5 0.6 collective-permute-done.refs_6_
  24.7 1.6 %collective-permute-start.4 = (bf16[64,1024]{1,0:T(8,128)(2,1)S(1)}, bf16[64,1024]{1,0:T(8,128)(2,1)S(1)}, u32[]{:S(2)}, u32[]{:S(2)}) collective-permute-start(bf16[64,1024]{1,0:T(8,128)(2,1)S(1)} %copy-done.5), channel_id=1, source_target_pairs={{0,32},{4,36},{8,40},{12,44},{16,48},{20,52},{24,56},{28,60},{32,0... | collective-permute-start | bytes 393224 | tf_op jit(solution)/shard_map/ppermute | solution.py:304
  26.3 2.9 %collective-permute-start.5 = (bf16[64,1024]{1,0:T(8,128)(2,1)S(1)}, bf16[64,1024]{1,0:T(8,128)(2,1)S(1)}, u32[]{:S(2)}, u32[]{:S(2)}) collective-permute-start(bf16[64,1024]{1,0:T(8,128)(2,1)S(1)} %copy-done.4), channel_id=1, source_target_pairs={{0,64},{4,68},{8,72},{12,76},{16,80},{20,84},{24,88},{28,92},{32,9... | collective-permute-start | bytes 393224 | tf_op jit(solution)/shard_map/ppermute | solution.py:304
  29.2 1.8 %collective-permute-done.4.refs_1_ = bf16[64,1024]{1,0:T(8,128)(2,1)S(1)} collective-permute-done((bf16[64,1024]{1,0:T(8,128)(2,1)S(1)}, bf16[64,1024]{1,0:T(8,128)(2,1)S(1)}, u32[]{:S(2)}, u32[]{:S(2)}) %collective-permute-start.4) | collective-permute-done | bytes 131104 | tf_op jit(solution)/shard_map/ppermute | solution.py:304
  31.0 3.0 %collective-permute-start.6 = (bf16[64,1024]{1,0:T(8,128)(2,1)S(1)}, bf16[64,1024]{1,0:T(8,128)(2,1)S(1)}, u32[]{:S(2)}, u32[]{:S(2)}) collective-permute-start(bf16[64,1024]{1,0:T(8,128)(2,1)S(1)} %copy-done.3), channel_id=1, source_target_pairs={{0,96},{4,100},{8,104},{12,108},{16,112},{20,116},{24,120},{28,124... | collective-permute-start | bytes 393224 | tf_op jit(solution)/shard_map/ppermute | solution.py:304
  34.1 1.9 %collective-permute-done.5.refs_2_ = bf16[64,1024]{1,0:T(8,128)(2,1)S(1)} collective-permute-done((bf16[64,1024]{1,0:T(8,128)(2,1)S(1)}, bf16[64,1024]{1,0:T(8,128)(2,1)S(1)}, u32[]{:S(2)}, u32[]{:S(2)}) %collective-permute-start.5) | collective-permute-done | bytes 131104 | tf_op jit(solution)/shard_map/ppermute | solution.py:304
  35.9 2.7 %collective-permute-done.6.refs_3_ = bf16[64,1024]{1,0:T(8,128)(2,1)S(1)} collective-permute-done((bf16[64,1024]{1,0:T(8,128)(2,1)S(1)}, bf16[64,1024]{1,0:T(8,128)(2,1)S(1)}, u32[]{:S(2)}, u32[]{:S(2)}) %collective-permute-start.6) | collective-permute-done | bytes 131104 | tf_op jit(solution)/shard_map/ppermute | solution.py:304
  38.7 1.7 %shard_map.110.refs_0_ = f32[128,128]{1,0:T(8,128)S(1)} custom-call(bf16[64,1024]{1,0:T(8,128)(2,1)S(1)} %copy-done, bf16[64,1024]{1,0:T(8,128)(2,1)S(1)} %collective-permute-done.4.refs_1_, bf16[64,1024]{1,0:T(8,128)(2,1)S(1)} %collective-permute-done.5.refs_2_, bf16[64,1024]{1,0:T(8,128)(2,1)S(1)} %collective-permute-done.6.refs_3_, ...), custom_call_target="tpu_custom_call" | custom-call | tf_op jit(solution)/shard_map/pallas_call | solution.py:200
  40.4 2.8 %collective-permute-start.12 = (f32[128,128]{1,0:T(8,128)S(1)}, f32[128,128]{1,0:T(8,128)S(1)}, u32[]{:S(2)}, u32[]{:S(2)}) collective-permute-start(f32[128,128]{1,0:T(8,128)S(1)} %shard_map.110.refs_0_), channel_id=1, source_target_pairs={{0,3},{1,2},{2,1},{3,0},{4,7},{5,6},{6,5},{7,4},{8,11},{9,10},{10,... | collective-permute-start | bytes 196616 | tf_op jit(solution)/shard_map/ppermute | solution.py:300
  43.2 0.8 %collective-permute-start.11 = (f32[128,128]{1,0:T(8,128)S(1)}, f32[128,128]{1,0:T(8,128)S(1)}, u32[]{:S(2)}, u32[]{:S(2)}) collective-permute-start(f32[128,128]{1,0:T(8,128)S(1)} %shard_map.110.refs_0_), channel_id=1, source_target_pairs={{0,2},{1,3},{2,0},{3,1},{4,6},{5,7},{6,4},{7,5},{8,10},{9,11},{10,... | collective-permute-start | bytes 196616 | tf_op jit(solution)/shard_map/ppermute | solution.py:300
  44.7 1.2 %collective-permute-done.12.refs_3_ = f32[128,128]{1,0:T(8,128)S(1)} collective-permute-done((f32[128,128]{1,0:T(8,128)S(1)}, f32[128,128]{1,0:T(8,128)S(1)}, u32[]{:S(2)}, u32[]{:S(2)}) %collective-permute-start.12) | collective-permute-done | bytes 65568 | tf_op jit(solution)/shard_map/ppermute | solution.py:300
  45.9 3.2 %collective-permute-done.11.refs_2_ = f32[128,128]{1,0:T(8,128)S(1)} collective-permute-done((f32[128,128]{1,0:T(8,128)S(1)}, f32[128,128]{1,0:T(8,128)S(1)}, u32[]{:S(2)}, u32[]{:S(2)}) %collective-permute-start.11) | collective-permute-done | bytes 65568 | tf_op jit(solution)/shard_map/ppermute | solution.py:300
  49.1 2.0 %shard_map.112 = (bf16[64,2048]{1,0:T(8,128)(2,1)S(1)}, bf16[64,2048]{1,0:T(8,128)(2,1)S(1)}, bf16[64,2048]{1,0:T(8,128)(2,1)S(1)}, bf16[64,2048]{1,0:T(8,128)(2,1)S(1)}) custom-call(f32[128,128]{1,0:T(8,128)S(1)} %shard_map.110.refs_0_, f32[128,128]{1,0:T(8,128)S(1)} %collective-permute-done.10.refs_1_, f32[128,128]{1,0:T(8,128)S(1)} %collective-permute-done.11.refs_2_, ...), custom_call_target="tpu_custom_call" | custom-call | tf_op jit(solution)/shard_map/pallas_call | solution.py:239
  51.4 2.7 %collective-permute-start.14 = (bf16[64,2048]{1,0:T(8,128)(2,1)S(1)}, bf16[64,2048]{1,0:T(8,128)(2,1)S(1)}, u32[]{:S(2)}, u32[]{:S(2)}) collective-permute-start(bf16[64,2048]{1,0:T(8,128)(2,1)S(1)} %get-tuple-element.49), channel_id=1, source_target_pairs={{0,64},{4,68},{8,72},{12,76},{16,80},{20,84},{24,88},{28,92},{32,9... | collective-permute-start | bytes 786440 | tf_op jit(solution)/shard_map/ppermute | solution.py:304
  54.0 1.9 %collective-permute-start.15 = (bf16[64,2048]{1,0:T(8,128)(2,1)S(1)}, bf16[64,2048]{1,0:T(8,128)(2,1)S(1)}, u32[]{:S(2)}, u32[]{:S(2)}) collective-permute-start(bf16[64,2048]{1,0:T(8,128)(2,1)S(1)} %get-tuple-element.50), channel_id=1, source_target_pairs={{0,96},{4,100},{8,104},{12,108},{16,112},{20,116},{24,120},{28,124... | collective-permute-start | bytes 786440 | tf_op jit(solution)/shard_map/ppermute | solution.py:304
  55.9 8.4 %shard_map.111 = f32[128,2048]{1,0:T(8,128)S(1)} custom-call(bf16[4,128,1024]{2,1,0:T(8,128)(2,1)} %all-to-all-done.piece_hbm, bf16[4096,2048]{1,0:T(8,128)(2,1)} %weight_hbm.1), custom_call_target="tpu_custom_call" | custom-call | flops 2147483648 | bytes 16777216 | tf_op jit(solution)/shard_map/pallas_call | solution.py:279
  64.3 1.6 %collective-permute-done.15 = bf16[64,2048]{1,0:T(8,128)(2,1)S(1)} collective-permute-done((bf16[64,2048]{1,0:T(8,128)(2,1)S(1)}, bf16[64,2048]{1,0:T(8,128)(2,1)S(1)}, u32[]{:S(2)}, u32[]{:S(2)}) %collective-permute-start.15) | collective-permute-done | bytes 262176 | tf_op jit(solution)/shard_map/ppermute | solution.py:304
  66.2 0.9 %add_convert_fusion = bf16[128,2048]{1,0:T(8,128)(2,1)} fusion(f32[128,2048]{1,0:T(8,128)S(1)} %shard_map.111, f32[128,2048]{1,0:T(8,128)S(1)} %fusion), kind=kLoop, calls=%fused_computation.8 | loop fusion | flops 524288 | bytes 2621440 | tf_op jit(solution)/shard_map/convert_element_type | solution.py:381
  (32 shorter events, 2.0 us)
Async XLA Ops:
  1.0 21.0 %collective-permute-start.3 = (bf16[64,3072]{1,0:T(8,128)(2,1)S(1)}, bf16[64,3072]{1,0:T(8,128)(2,1)S(1)}, u32[]{:S(2)}, u32[]{:S(2)}) collective-permute-start(bf16[64,3072]{1,0:T(8,128)(2,1)S(1)} %pad_maximum_fusion.refs_4_), channel_id=1, source_target_pairs={{0,4},{4,0},{8,12},{12,8},{16,20},{20,16},{24,28},{28,24},{32,36},... | collective-permute-start | bytes 1179656 | tf_op jit(solution)/shard_map/ppermute | solution.py:304
  1.1 22.4 %collective-permute-start.2 = (bf16[64,3072]{1,0:T(8,128)(2,1)S(1)}, bf16[64,3072]{1,0:T(8,128)(2,1)}, u32[]{:S(2)}, u32[]{:S(2)}) collective-permute-start(bf16[64,3072]{1,0:T(8,128)(2,1)S(1)} %pad_maximum_fusion.refs_4_), channel_id=1, source_target_pairs={{0,24},{4,28},{8,16},{12,20},{16,8},{20,12},{24,0},{28,4},{32,56},... | collective-permute-start | bytes 1179656 | tf_op jit(solution)/shard_map/ppermute | solution.py:304
  5.3 18.2 %collective-permute-start.1 = (bf16[64,3072]{1,0:T(8,128)(2,1)S(1)}, bf16[64,3072]{1,0:T(8,128)(2,1)}, u32[]{:S(2)}, u32[]{:S(2)}) collective-permute-start(bf16[64,3072]{1,0:T(8,128)(2,1)S(1)} %pad_maximum_fusion.refs_4_), channel_id=1, source_target_pairs={{0,16},{4,20},{8,24},{12,28},{16,0},{20,4},{24,8},{28,12},{32,48},... | collective-permute-start | bytes 1179656 | tf_op jit(solution)/shard_map/ppermute | solution.py:304
  5.3 18.8 %collective-permute-start = (bf16[64,3072]{1,0:T(8,128)(2,1)S(1)}, bf16[64,3072]{1,0:T(8,128)(2,1)}, u32[]{:S(2)}, u32[]{:S(2)}) collective-permute-start(bf16[64,3072]{1,0:T(8,128)(2,1)S(1)} %pad_maximum_fusion.refs_4_), channel_id=1, source_target_pairs={{0,8},{4,12},{8,0},{12,4},{16,24},{20,28},{24,16},{28,20},{32,40},... | collective-permute-start | bytes 1179656 | tf_op jit(solution)/shard_map/ppermute | solution.py:304
  17.6 7.1 %copy-start.5 = (bf16[64,1024]{1,0:T(8,128)(2,1)S(1)}, bf16[64,1024]{1,0:T(8,128)(2,1)}, u32[]{:S(2)}) copy-start(bf16[64,1024]{1,0:T(8,128)(2,1)} %get-tuple-element.33) | copy-start | bytes 393220
  17.6 8.7 %copy-start.4 = (bf16[64,1024]{1,0:T(8,128)(2,1)S(1)}, bf16[64,1024]{1,0:T(8,128)(2,1)}, u32[]{:S(2)}) copy-start(bf16[64,1024]{1,0:T(8,128)(2,1)} %get-tuple-element.34) | copy-start | bytes 393220
  17.6 13.4 %copy-start.3 = (bf16[64,1024]{1,0:T(8,128)(2,1)S(1)}, bf16[64,1024]{1,0:T(8,128)(2,1)}, u32[]{:S(2)}) copy-start(bf16[64,1024]{1,0:T(8,128)(2,1)} %get-tuple-element.35) | copy-start | bytes 393220
  17.6 16.4 %copy-start.1 = (s32[32]{0:T(128)S(1)}, s32[32]{0:T(128)}, u32[]{:S(2)}) copy-start(s32[32]{0:T(128)} %refs_1_.1) | copy-start | bytes 388
  17.6 16.4 %copy-start.2 = (s32[128]{0:T(128)S(1)}, s32[128]{0:T(128)}, u32[]{:S(2)}) copy-start(s32[128]{0:T(128)} %param.18) | copy-start | bytes 1540
  17.6 21.1 %copy-start = (bf16[64,1024]{1,0:T(8,128)(2,1)S(1)}, bf16[64,1024]{1,0:T(8,128)(2,1)}, u32[]{:S(2)}) copy-start(bf16[64,1024]{1,0:T(8,128)(2,1)} %get-tuple-element.32.refs_0_) | copy-start | bytes 393220
  17.6 27.1 %all-to-all-start = ((bf16[4,128,1024]{2,1,0:T(8,128)(2,1)}), bf16[4,128,1024]{2,1,0:T(8,128)(2,1)}, u32[]{:S(2)}, u32[]{:S(2)}) async-start(bf16[4,128,1024]{2,1,0:T(8,128)(2,1)} %get-tuple-element.40), calls=%async_computation | async-start | bytes 2097152 | tf_op jit(solution)/shard_map/all_to_all | solution.py:354
  24.2 14.5 %collective-permute-start.7 = (bf16[64,3072]{1,0:T(8,128)(2,1)}, bf16[64,3072]{1,0:T(8,128)(2,1)S(1)}, u32[]{:S(2)}, u32[]{:S(2)}) collective-permute-start(bf16[64,3072]{1,0:T(8,128)(2,1)} %collective-permute-done.refs_6_), channel_id=1, source_target_pairs={{0,4},{4,0},{8,12},{12,8},{16,20},{20,16},{24,28},{28,24},{32,36},... | collective-permute-start | bytes 1179656 | tf_op jit(solution)/shard_map/ppermute | solution.py:304
  24.2 14.5 %collective-permute-start.8 = (bf16[64,3072]{1,0:T(8,128)(2,1)}, bf16[64,3072]{1,0:T(8,128)(2,1)S(1)}, u32[]{:S(2)}, u32[]{:S(2)}) collective-permute-start(bf16[64,3072]{1,0:T(8,128)(2,1)} %collective-permute-done.1.refs_8_), channel_id=1, source_target_pairs={{0,4},{4,0},{8,12},{12,8},{16,20},{20,16},{24,28},{28,24},{32,36},... | collective-permute-start | bytes 1179656 | tf_op jit(solution)/shard_map/ppermute | solution.py:304
  24.7 14.0 %collective-permute-start.9 = (bf16[64,3072]{1,0:T(8,128)(2,1)}, bf16[64,3072]{1,0:T(8,128)(2,1)S(1)}, u32[]{:S(2)}, u32[]{:S(2)}) collective-permute-start(bf16[64,3072]{1,0:T(8,128)(2,1)} %collective-permute-done.2.refs_10_), channel_id=1, source_target_pairs={{0,4},{4,0},{8,12},{12,8},{16,20},{20,16},{24,28},{28,24},{32,36},... | collective-permute-start | bytes 1179656 | tf_op jit(solution)/shard_map/ppermute | solution.py:304
  24.7 6.3 %collective-permute-start.4 = (bf16[64,1024]{1,0:T(8,128)(2,1)S(1)}, bf16[64,1024]{1,0:T(8,128)(2,1)S(1)}, u32[]{:S(2)}, u32[]{:S(2)}) collective-permute-start(bf16[64,1024]{1,0:T(8,128)(2,1)S(1)} %copy-done.5), channel_id=1, source_target_pairs={{0,32},{4,36},{8,40},{12,44},{16,48},{20,52},{24,56},{28,60},{32,0... | collective-permute-start | bytes 393224 | tf_op jit(solution)/shard_map/ppermute | solution.py:304
  26.3 9.7 %collective-permute-start.5 = (bf16[64,1024]{1,0:T(8,128)(2,1)S(1)}, bf16[64,1024]{1,0:T(8,128)(2,1)S(1)}, u32[]{:S(2)}, u32[]{:S(2)}) collective-permute-start(bf16[64,1024]{1,0:T(8,128)(2,1)S(1)} %copy-done.4), channel_id=1, source_target_pairs={{0,64},{4,68},{8,72},{12,76},{16,80},{20,84},{24,88},{28,92},{32,9... | collective-permute-start | bytes 393224 | tf_op jit(solution)/shard_map/ppermute | solution.py:304
  31.0 7.7 %collective-permute-start.6 = (bf16[64,1024]{1,0:T(8,128)(2,1)S(1)}, bf16[64,1024]{1,0:T(8,128)(2,1)S(1)}, u32[]{:S(2)}, u32[]{:S(2)}) collective-permute-start(bf16[64,1024]{1,0:T(8,128)(2,1)S(1)} %copy-done.3), channel_id=1, source_target_pairs={{0,96},{4,100},{8,104},{12,108},{16,112},{20,116},{24,120},{28,124... | collective-permute-start | bytes 393224 | tf_op jit(solution)/shard_map/ppermute | solution.py:304
  40.4 5.5 %collective-permute-start.12 = (f32[128,128]{1,0:T(8,128)S(1)}, f32[128,128]{1,0:T(8,128)S(1)}, u32[]{:S(2)}, u32[]{:S(2)}) collective-permute-start(f32[128,128]{1,0:T(8,128)S(1)} %shard_map.110.refs_0_), channel_id=1, source_target_pairs={{0,3},{1,2},{2,1},{3,0},{4,7},{5,6},{6,5},{7,4},{8,11},{9,10},{10,... | collective-permute-start | bytes 196616 | tf_op jit(solution)/shard_map/ppermute | solution.py:300
  43.2 5.9 %collective-permute-start.11 = (f32[128,128]{1,0:T(8,128)S(1)}, f32[128,128]{1,0:T(8,128)S(1)}, u32[]{:S(2)}, u32[]{:S(2)}) collective-permute-start(f32[128,128]{1,0:T(8,128)S(1)} %shard_map.110.refs_0_), channel_id=1, source_target_pairs={{0,2},{1,3},{2,0},{3,1},{4,6},{5,7},{6,4},{7,5},{8,10},{9,11},{10,... | collective-permute-start | bytes 196616 | tf_op jit(solution)/shard_map/ppermute | solution.py:300
  44.0 5.1 %collective-permute-start.10 = (f32[128,128]{1,0:T(8,128)S(1)}, f32[128,128]{1,0:T(8,128)S(1)}, u32[]{:S(2)}, u32[]{:S(2)}) collective-permute-start(f32[128,128]{1,0:T(8,128)S(1)} %shard_map.110.refs_0_), channel_id=1, source_target_pairs={{0,1},{1,0},{2,3},{3,2},{4,5},{5,4},{6,7},{7,6},{8,9},{9,8},{10,11... | collective-permute-start | bytes 196616 | tf_op jit(solution)/shard_map/ppermute | solution.py:300
  51.1 13.2 %collective-permute-start.13 = (bf16[64,2048]{1,0:T(8,128)(2,1)S(1)}, bf16[64,2048]{1,0:T(8,128)(2,1)S(1)}, u32[]{:S(2)}, u32[]{:S(2)}) collective-permute-start(bf16[64,2048]{1,0:T(8,128)(2,1)S(1)} %get-tuple-element.48), channel_id=1, source_target_pairs={{0,32},{4,36},{8,40},{12,44},{16,48},{20,52},{24,56},{28,60},{32,0... | collective-permute-start | bytes 786440 | tf_op jit(solution)/shard_map/ppermute | solution.py:304
  51.4 12.9 %collective-permute-start.14 = (bf16[64,2048]{1,0:T(8,128)(2,1)S(1)}, bf16[64,2048]{1,0:T(8,128)(2,1)S(1)}, u32[]{:S(2)}, u32[]{:S(2)}) collective-permute-start(bf16[64,2048]{1,0:T(8,128)(2,1)S(1)} %get-tuple-element.49), channel_id=1, source_target_pairs={{0,64},{4,68},{8,72},{12,76},{16,80},{20,84},{24,88},{28,92},{32,9... | collective-permute-start | bytes 786440 | tf_op jit(solution)/shard_map/ppermute | solution.py:304
  54.0 11.9 %collective-permute-start.15 = (bf16[64,2048]{1,0:T(8,128)(2,1)S(1)}, bf16[64,2048]{1,0:T(8,128)(2,1)S(1)}, u32[]{:S(2)}, u32[]{:S(2)}) collective-permute-start(bf16[64,2048]{1,0:T(8,128)(2,1)S(1)} %get-tuple-element.50), channel_id=1, source_target_pairs={{0,96},{4,100},{8,104},{12,108},{16,112},{20,116},{24,120},{28,124... | collective-permute-start | bytes 786440 | tf_op jit(solution)/shard_map/ppermute | solution.py:304

commit v3 on v2

--- a/solution.py
+++ b/solution.py
@@ -19,6 +19,8 @@
 BLOCK = 32
 ATTEND_VMEM = 63 * 2**20
 STAGED = 6
+AHEAD = 2
+PROJECT_AHEAD = 3
 DEPTH = 512
 
 
@@ -42,10 +44,10 @@
     attended_ref, bucket_refs, refs = refs[0], refs[1 : 1 + RING], refs[1 + RING :]
     staged, refs = refs[:STAGED], refs[STAGED:]
     length_ref, table_ref, adapter_ref, query_ref, token_key_ref, token_value_ref = staged
-    key_ref, value_ref, heads_ref, fresh_key_ref, fresh_value_ref, mixed_ref, used_ref = refs[:7]
-    staged_sem, key_sem, value_sem = refs[7:]
+    key_ref, value_ref, heads_ref, mixed_ref, staged_sem, key_sem, value_sem = refs
     f32, bf16 = jnp.float32, jnp.bfloat16
     requests, positions, _ = key_ref.shape
+    blocks = requests // BLOCK
     score_scale = 1.0 / math.sqrt(HEAD_DIM)
 
     def fetch(source, target, sem, c):
@@ -58,51 +60,55 @@
     ]
     for copy in staging:
         copy.start()
-    for c in range(requests // BLOCK):
+    def start(c):
         fetch(key_hbm, key_ref, key_sem, c).start()
         fetch(value_hbm, value_ref, value_sem, c).start()
+
+    for c in range(min(AHEAD, blocks)):
+        start(c)
     for copy in staging:
         copy.wait()
     slots_at = slot_positions(adapter_ref[...], table_ref)
 
-    for c in range(requests // BLOCK):
+    for c in range(blocks):
+        if c + AHEAD < blocks:
+            start(c + AHEAD)
         rows = slice(c * BLOCK, (c + 1) * BLOCK)
-        fresh_keys = token_key_ref[rows, :].astype(f32)
-        fresh_values = token_value_ref[rows, :].astype(f32)
         for h in range(GROUP):
-            at = pl.ds(h, BLOCK, stride=GROUP)
-            heads_ref[at, :] = query_ref[rows, h * HEAD_DIM : (h + 1) * HEAD_DIM].astype(f32)
-            fresh_key_ref[at, :] = fresh_keys
-            fresh_value_ref[at, :] = fresh_values
-        for r in range(BLOCK):
-            used_ref[r * GROUP : (r + 1) * GROUP, :] = jnp.full(
-                (GROUP, positions), length_ref[c * BLOCK + r], jnp.int32
-            )
-        heads = heads_ref[...]
+            heads_ref[pl.ds(h, BLOCK, stride=GROUP), :] = query_ref[
+                rows, h * HEAD_DIM : (h + 1) * HEAD_DIM
+            ].astype(f32)
+        heads = heads_ref[...].reshape(BLOCK, GROUP, HEAD_DIM)
+        fresh_keys = token_key_ref[rows, :].astype(f32)[:, None, :]
+        fresh_values = token_value_ref[rows, :].astype(f32)[:, None, :]
         fetch(key_hbm, key_ref, key_sem, c).wait()
-        score = lax.dot_general(
-            heads.reshape(BLOCK, GROUP, HEAD_DIM).astype(bf16),
+        score = score_scale * lax.dot_general(
+            heads.astype(bf16),
             key_ref[rows],
             (((2,), (2,)), ((0,), (0,))),
             preferred_element_type=f32,
         )
-        score = score.reshape(BLOCK * GROUP, positions) * score_scale
-        fresh = jnp.sum(heads * fresh_key_ref[...], axis=1, keepdims=True) * score_scale
-        place = lax.broadcasted_iota(jnp.int32, score.shape, 1)
-        score = jnp.where(place < used_ref[...], score, -jnp.inf)
-        row_max = jnp.maximum(jnp.max(score, axis=1, keepdims=True), fresh)
+        fresh = jnp.sum(heads * fresh_keys, axis=2, keepdims=True) * score_scale
+        place = lax.broadcasted_iota(jnp.int32, (GROUP, positions), 1)
+        score = jnp.stack(
+            [
+                jnp.where(place < length_ref[c * BLOCK + r], score[r], -jnp.inf)
+                for r in range(BLOCK)
+            ]
+        )
+        row_max = jnp.maximum(jnp.max(score, axis=2, keepdims=True), fresh)
         weight = jnp.exp(score - row_max)
         fresh_weight = jnp.exp(fresh - row_max)
-        weight_sum = jnp.sum(weight, axis=1, keepdims=True) + fresh_weight
+        weight_sum = jnp.sum(weight, axis=2, keepdims=True) + fresh_weight
         fetch(value_hbm, value_ref, value_sem, c).wait()
         mixed = lax.dot_general(
-            weight.reshape(BLOCK, GROUP, positions).astype(bf16),
+            weight.astype(bf16),
             value_ref[rows],
             (((2,), (1,)), ((0,), (0,))),
             preferred_element_type=f32,
-        ).reshape(BLOCK * GROUP, HEAD_DIM)
-        mixed = mixed + fresh_weight.astype(bf16).astype(f32) * fresh_value_ref[...]
-        mixed_ref[...] = mixed / weight_sum
+        )
+        mixed = mixed + fresh_weight.astype(bf16).astype(f32) * fresh_values
+        mixed_ref[...] = (mixed / weight_sum).reshape(BLOCK * GROUP, HEAD_DIM)
         for h in range(GROUP):
             attended_ref[0, rows, h * HEAD_DIM : (h + 1) * HEAD_DIM] = mixed_ref[
                 pl.ds(h, BLOCK, stride=GROUP), :
@@ -150,8 +156,7 @@
             pltpu.VMEM(token_values.shape, jnp.bfloat16),
         ]
         + [pltpu.VMEM(cached_key_rows.shape, jnp.bfloat16)] * 2
-        + [per_head] * 4
-        + [pltpu.VMEM((BLOCK * GROUP, positions), jnp.int32)]
+        + [per_head] * 2
         + [pltpu.SemaphoreType.DMA((STAGED,)), fetches, fetches],
         compiler_params=pltpu.CompilerParams(vmem_limit_bytes=ATTEND_VMEM),
         cost_estimate=pl.CostEstimate(
@@ -255,10 +260,13 @@
 
     pieces = pltpu.make_async_copy(piece_hbm, piece_ref, piece_sem)
     pieces.start()
-    for c in range(sem.shape[0]):
+    count = sem.shape[0]
+    for c in range(min(PROJECT_AHEAD, count)):
         fetch(c).start()
     pieces.wait()
-    for c in range(sem.shape[0]):
+    for c in range(count):
+        if c + PROJECT_AHEAD < count:
+            fetch(c + PROJECT_AHEAD).start()
         fetch(c).wait()
         piece, part = c // per_piece, c % per_piece
         product = jnp.dot(
@@ -337,7 +345,7 @@
 
     down_here, up_here = adapter_down_weight[0], adapter_up_weight[0]
     both = jnp.concatenate([down_here, up_here], axis=1)
-    over_z = [swap_z(both, k) for k in range(1, Z_CHIPS)]
+    beside = [swap_z(both, k) for k in (1, 3)]
     both_other = swap_core(both)
 
     attended, *placed = attend(
@@ -352,13 +360,18 @@
         owned * CAP,
     )
     pieces = lax.all_to_all(attended, "tensor", 0, 0)
-    placed, over_z, both_other, request_adapter = lax.optimization_barrier(
-        (placed, over_z, both_other, request_adapter)
+    placed, beside, both_late, request_adapter = lax.optimization_barrier(
+        (placed, beside, both, request_adapter)
+    )
+    across = swap_z(both_late, 2)
+    beside_other = [swap_core(w) for w in beside]
+    placed, beside_other, both_other = lax.optimization_barrier(
+        (placed, beside_other, both_other)
     )
     routed = [placed[0]] + [swap_y(placed[m], m) for m in range(1, RING)]
-    table = [both, both_other]
-    for w in over_z:
-        table += [w, swap_core(w)]
+    routed, across = lax.optimization_barrier((routed, across))
+    table = [both, both_other, beside[0], beside_other[0]]
+    table += [across, swap_core(across), beside[1], beside_other[1]]
 
     every_adapter = adapter_table_row.shape[0]
     matches = request_adapter[:, None] == jnp.arange(every_adapter, dtype=jnp.int32)[None, :]

time: 67.4 us -> 64.3 us (0.954)
  waiting for transfers between devices: 14.5 us -> 19.2 us
  Pallas kernels: 23.4 us -> 19.3 us
  starting transfers between devices: 26.6 us -> 22.9 us
    ppermute x13, waiting for transfers between devices: 10.1 us -> 14.7 us  [swap_dp(): lax.ppermute(value, 'dp', [(i, i ^ k) for i in range(RING * Z_CHIPS * COR...]
    ppermute x13, starting transfers between devices: 18 us -> 14.5 us  [swap_dp(): lax.ppermute(value, 'dp', [(i, i ^ k) for i in range(RING * Z_CHIPS * COR...]
    pallas_call x1, Pallas kernels: 11.3 us -> 8.55 us  [attend(): pl.pallas_call(attend_kernel, in_specs=[hbm] * (STAGED + 2), out_specs=[v...]
    pallas_call x1, Pallas kernels: 8.36 us -> 7.27 us  [project(): pl.pallas_call(project_kernel, in_specs=[hbm, hbm], out_specs=pl.BlockSpe...]
  transfers between devices with their start and end apart: 17 -> 17, of which waited for: 8 -> 10; matrix products, arithmetic and copies ran while one was open for 0% -> 0% of each run, Pallas kernels for 32% -> 27%
where the time goes in v3:
time: 64.3 us; the launch traced here: 64.1 us
  starting transfers between devices  22.9 us (36%)
  Pallas kernels  19.3 us (30%)
  waiting for transfers between devices  19.2 us (30%)
  other arithmetic  2.17 us (3%)
    ppermute x13, waiting for transfers between devices, swap_dp(): lax.ppermute(value, 'dp', [(i, i ^ k) for i in range(RING * Z_CHIPS * COR...  14.7 us
    ppermute x13, starting transfers between devices, swap_dp(): lax.ppermute(value, 'dp', [(i, i ^ k) for i in range(RING * Z_CHIPS * COR...  14.5 us
    pallas_call x1, Pallas kernels, attend(): pl.pallas_call(attend_kernel, in_specs=[hbm] * (STAGED + 2), out_specs=[v...  8.55 us
    pallas_call x1, Pallas kernels, project(): pl.pallas_call(project_kernel, in_specs=[hbm, hbm], out_specs=pl.BlockSpe...  7.27 us
    ppermute x3, waiting for transfers between devices, swap_tensor(): return lax.ppermute(value, 'tensor', [(i, i ^ k) for i in range(RING)])  4.49 us
    all_to_all x1, starting transfers between devices, on_device(): pieces = lax.all_to_all(attended, 'tensor', 0, 0)  4.29 us
    ppermute x3, starting transfers between devices, swap_tensor(): return lax.ppermute(value, 'tensor', [(i, i ^ k) for i in range(RING)])  4.12 us
    pallas_call x1, Pallas kernels, up(): pl.pallas_call(functools.partial(up_kernel, columns), in_specs=[vmem] * (...  1.88 us
  transfers between devices with their start and end apart: 17, of which 10 were waited for; matrix products, arithmetic and copies ran while one was open for 0% of the time, Pallas kernels for 27%

profile of v3, /device:TPU:0, one launch (start us, length us, event | category | flops | bytes accessed | tf_op | source)
XLA Modules:
  0.0 64.1 jit_solution(7854958200809989923)
XLA Ops:
  0.0 1.0 %pad_maximum_fusion.refs_4_ = bf16[64,3072]{1,0:T(8,128)(2,1)S(1)} fusion(bf16[64,2048]{1,0:T(8,128)(2,1)} %bitcast.3, bf16[64,1024]{1,0:T(8,128)(2,1)} %bitcast.4), kind=kLoop, calls=%fused_computation.9 | loop fusion | flops 786432 | bytes 786432 | tf_op jit(solution)/shard_map/concatenate | solution.py:347
  1.0 4.2 %collective-permute-start.1 = (bf16[64,3072]{1,0:T(8,128)(2,1)S(1)}, bf16[64,3072]{1,0:T(8,128)(2,1)S(1)}, u32[]{:S(2)}, u32[]{:S(2)}) collective-permute-start(bf16[64,3072]{1,0:T(8,128)(2,1)S(1)} %pad_maximum_fusion.refs_4_), channel_id=1, source_target_pairs={{0,24},{4,28},{8,16},{12,20},{16,8},{20,12},{24,0},{28,4},{32,56},... | collective-permute-start | bytes 1179656 | tf_op jit(solution)/shard_map/ppermute | solution.py:312
  5.2 8.6 %shard_map.109 = (bf16[4,128,1024]{2,1,0:T(8,128)(2,1)}, bf16[64,1024]{1,0:T(8,128)(2,1)}, bf16[64,1024]{1,0:T(8,128)(2,1)}, bf16[64,1024]{1,0:T(8,128)(2,1)}, bf16[64,1024]{1,0:T(8,128)(2,1)}) custom-call(s32[128]{0:T(128)} %refs_0_.1, s32[32]{0:T(128)} %refs_1_.1, s32[1,128]{1,0:T(1,128)} %bitcast.5, bf16[128,1024]{1,0:T(8,128)(2,1)} %refs_3_.1, ...), custom_call_target="tpu_custom_call" | custom-call | flops 134217728 | bytes 16777216 | tf_op jit(solution)/shard_map/pallas_call | solution.py:144
  14.3 1.6 %collective-permute-done.refs_6_ = bf16[64,3072]{1,0:T(8,128)(2,1)} collective-permute-done((bf16[64,3072]{1,0:T(8,128)(2,1)S(1)}, bf16[64,3072]{1,0:T(8,128)(2,1)}, u32[]{:S(2)}, u32[]{:S(2)}) %collective-permute-start) | collective-permute-done | bytes 393248 | tf_op jit(solution)/shard_map/ppermute | solution.py:312
  16.6 4.3 %all-to-all-start = ((bf16[4,128,1024]{2,1,0:T(8,128)(2,1)}), bf16[4,128,1024]{2,1,0:T(8,128)(2,1)}, u32[]{:S(2)}, u32[]{:S(2)}) async-start(bf16[4,128,1024]{2,1,0:T(8,128)(2,1)} %get-tuple-element.62), calls=%async_computation | async-start | bytes 2097152 | tf_op jit(solution)/shard_map/all_to_all | solution.py:362
  20.9 1.7 %collective-permute-start.5 = (bf16[64,1024]{1,0:T(8,128)(2,1)S(1)}, bf16[64,1024]{1,0:T(8,128)(2,1)S(1)}, u32[]{:S(2)}, u32[]{:S(2)}) collective-permute-start(bf16[64,1024]{1,0:T(8,128)(2,1)S(1)} %copy-done.5), channel_id=1, source_target_pairs={{0,32},{4,36},{8,40},{12,44},{16,48},{20,52},{24,56},{28,60},{32,0... | collective-permute-start | bytes 393224 | tf_op jit(solution)/shard_map/ppermute | solution.py:312
  22.6 2.9 %collective-permute-start.6 = (bf16[64,1024]{1,0:T(8,128)(2,1)S(1)}, bf16[64,1024]{1,0:T(8,128)(2,1)S(1)}, u32[]{:S(2)}, u32[]{:S(2)}) collective-permute-start(bf16[64,1024]{1,0:T(8,128)(2,1)S(1)} %copy-done.4), channel_id=1, source_target_pairs={{0,64},{4,68},{8,72},{12,76},{16,80},{20,84},{24,88},{28,92},{32,9... | collective-permute-start | bytes 393224 | tf_op jit(solution)/shard_map/ppermute | solution.py:312
  25.7 3.2 %collective-permute-done.8.refs_8_ = bf16[64,3072]{1,0:T(8,128)(2,1)S(1)} collective-permute-done((bf16[64,3072]{1,0:T(8,128)(2,1)S(1)}, bf16[64,3072]{1,0:T(8,128)(2,1)S(1)}, u32[]{:S(2)}, u32[]{:S(2)}) %collective-permute-start.8) | collective-permute-done | bytes 393248 | tf_op jit(solution)/shard_map/ppermute | solution.py:312
  28.9 2.6 %collective-permute-done.6.refs_2_ = bf16[64,1024]{1,0:T(8,128)(2,1)S(1)} collective-permute-done((bf16[64,1024]{1,0:T(8,128)(2,1)S(1)}, bf16[64,1024]{1,0:T(8,128)(2,1)S(1)}, u32[]{:S(2)}, u32[]{:S(2)}) %collective-permute-start.6) | collective-permute-done | bytes 131104 | tf_op jit(solution)/shard_map/ppermute | solution.py:312
  31.6 2.0 %collective-permute-done.7.refs_3_ = bf16[64,1024]{1,0:T(8,128)(2,1)S(1)} collective-permute-done((bf16[64,1024]{1,0:T(8,128)(2,1)S(1)}, bf16[64,1024]{1,0:T(8,128)(2,1)S(1)}, u32[]{:S(2)}, u32[]{:S(2)}) %collective-permute-start.7) | collective-permute-done | bytes 131104 | tf_op jit(solution)/shard_map/ppermute | solution.py:312
  33.7 1.6 %collective-permute-done.9.refs_9_ = bf16[64,3072]{1,0:T(8,128)(2,1)S(1)} collective-permute-done((bf16[64,3072]{1,0:T(8,128)(2,1)S(1)}, bf16[64,3072]{1,0:T(8,128)(2,1)S(1)}, u32[]{:S(2)}, u32[]{:S(2)}) %collective-permute-start.9) | collective-permute-done | bytes 393248 | tf_op jit(solution)/shard_map/ppermute | solution.py:312
  35.3 1.6 %shard_map.110.refs_0_ = f32[128,128]{1,0:T(8,128)S(1)} custom-call(bf16[64,1024]{1,0:T(8,128)(2,1)S(1)} %copy-done, bf16[64,1024]{1,0:T(8,128)(2,1)S(1)} %collective-permute-done.5.refs_1_, bf16[64,1024]{1,0:T(8,128)(2,1)S(1)} %collective-permute-done.6.refs_2_, bf16[64,1024]{1,0:T(8,128)(2,1)S(1)} %collective-permute-done.7.refs_3_, ...), custom_call_target="tpu_custom_call" | custom-call | tf_op jit(solution)/shard_map/pallas_call | solution.py:205
  36.9 2.7 %collective-permute-start.12 = (f32[128,128]{1,0:T(8,128)S(1)}, f32[128,128]{1,0:T(8,128)S(1)}, u32[]{:S(2)}, u32[]{:S(2)}) collective-permute-start(f32[128,128]{1,0:T(8,128)S(1)} %shard_map.110.refs_0_), channel_id=1, source_target_pairs={{0,3},{1,2},{2,1},{3,0},{4,7},{5,6},{6,5},{7,4},{8,11},{9,10},{10,... | collective-permute-start | bytes 196616 | tf_op jit(solution)/shard_map/ppermute | solution.py:308
  39.6 0.8 %collective-permute-start.11 = (f32[128,128]{1,0:T(8,128)S(1)}, f32[128,128]{1,0:T(8,128)S(1)}, u32[]{:S(2)}, u32[]{:S(2)}) collective-permute-start(f32[128,128]{1,0:T(8,128)S(1)} %shard_map.110.refs_0_), channel_id=1, source_target_pairs={{0,2},{1,3},{2,0},{3,1},{4,6},{5,7},{6,4},{7,5},{8,10},{9,11},{10,... | collective-permute-start | bytes 196616 | tf_op jit(solution)/shard_map/ppermute | solution.py:308
  40.5 0.5 collective-permute-start.10
  41.2 1.2 %collective-permute-done.12.refs_3_ = f32[128,128]{1,0:T(8,128)S(1)} collective-permute-done((f32[128,128]{1,0:T(8,128)S(1)}, f32[128,128]{1,0:T(8,128)S(1)}, u32[]{:S(2)}, u32[]{:S(2)}) %collective-permute-start.12) | collective-permute-done | bytes 65568 | tf_op jit(solution)/shard_map/ppermute | solution.py:308
  42.4 3.3 %collective-permute-done.11.refs_2_ = f32[128,128]{1,0:T(8,128)S(1)} collective-permute-done((f32[128,128]{1,0:T(8,128)S(1)}, f32[128,128]{1,0:T(8,128)S(1)}, u32[]{:S(2)}, u32[]{:S(2)}) %collective-permute-start.11) | collective-permute-done | bytes 65568 | tf_op jit(solution)/shard_map/ppermute | solution.py:308
  45.7 1.9 %shard_map.112 = (bf16[64,2048]{1,0:T(8,128)(2,1)S(1)}, bf16[64,2048]{1,0:T(8,128)(2,1)S(1)}, bf16[64,2048]{1,0:T(8,128)(2,1)S(1)}, bf16[64,2048]{1,0:T(8,128)(2,1)S(1)}) custom-call(f32[128,128]{1,0:T(8,128)S(1)} %shard_map.110.refs_0_, f32[128,128]{1,0:T(8,128)S(1)} %collective-permute-done.10.refs_1_, f32[128,128]{1,0:T(8,128)S(1)} %collective-permute-done.11.refs_2_, ...), custom_call_target="tpu_custom_call" | custom-call | tf_op jit(solution)/shard_map/pallas_call | solution.py:244
  47.7 2.2 %collective-permute-start.14 = (bf16[64,2048]{1,0:T(8,128)(2,1)S(1)}, bf16[64,2048]{1,0:T(8,128)(2,1)S(1)}, u32[]{:S(2)}, u32[]{:S(2)}) collective-permute-start(bf16[64,2048]{1,0:T(8,128)(2,1)S(1)} %get-tuple-element.71), channel_id=1, source_target_pairs={{0,64},{4,68},{8,72},{12,76},{16,80},{20,84},{24,88},{28,92},{32,9... | collective-permute-start | bytes 786440 | tf_op jit(solution)/shard_map/ppermute | solution.py:312
  49.9 2.4 %collective-permute-start.15 = (bf16[64,2048]{1,0:T(8,128)(2,1)S(1)}, bf16[64,2048]{1,0:T(8,128)(2,1)S(1)}, u32[]{:S(2)}, u32[]{:S(2)}) collective-permute-start(bf16[64,2048]{1,0:T(8,128)(2,1)S(1)} %get-tuple-element.72), channel_id=1, source_target_pairs={{0,96},{4,100},{8,104},{12,108},{16,112},{20,116},{24,120},{28,124... | collective-permute-start | bytes 786440 | tf_op jit(solution)/shard_map/ppermute | solution.py:312
  52.4 7.3 %shard_map.111 = f32[128,2048]{1,0:T(8,128)S(1)} custom-call(bf16[4,128,1024]{2,1,0:T(8,128)(2,1)} %all-to-all-done.piece_hbm, bf16[4096,2048]{1,0:T(8,128)(2,1)} %weight_hbm.1), custom_call_target="tpu_custom_call" | custom-call | flops 2147483648 | bytes 16777216 | tf_op jit(solution)/shard_map/pallas_call | solution.py:287
  59.7 0.6 collective-permute-done.14
  60.2 2.6 %collective-permute-done.15 = bf16[64,2048]{1,0:T(8,128)(2,1)S(1)} collective-permute-done((bf16[64,2048]{1,0:T(8,128)(2,1)S(1)}, bf16[64,2048]{1,0:T(8,128)(2,1)S(1)}, u32[]{:S(2)}, u32[]{:S(2)}) %collective-permute-start.15) | collective-permute-done | bytes 262176 | tf_op jit(solution)/shard_map/ppermute | solution.py:312
  63.2 0.9 %add_convert_fusion = bf16[128,2048]{1,0:T(8,128)(2,1)} fusion(f32[128,2048]{1,0:T(8,128)S(1)} %shard_map.111, f32[128,2048]{1,0:T(8,128)S(1)} %fusion), kind=kLoop, calls=%fused_computation.8 | loop fusion | flops 524288 | bytes 2621440 | tf_op jit(solution)/shard_map/convert_element_type | solution.py:394
  (32 shorter events, 2.2 us)
Async XLA Ops:
  1.0 13.3 %collective-permute-start.1 = (bf16[64,3072]{1,0:T(8,128)(2,1)S(1)}, bf16[64,3072]{1,0:T(8,128)(2,1)S(1)}, u32[]{:S(2)}, u32[]{:S(2)}) collective-permute-start(bf16[64,3072]{1,0:T(8,128)(2,1)S(1)} %pad_maximum_fusion.refs_4_), channel_id=1, source_target_pairs={{0,24},{4,28},{8,16},{12,20},{16,8},{20,12},{24,0},{28,4},{32,56},... | collective-permute-start | bytes 1179656 | tf_op jit(solution)/shard_map/ppermute | solution.py:312
  5.2 10.7 %collective-permute-start = (bf16[64,3072]{1,0:T(8,128)(2,1)S(1)}, bf16[64,3072]{1,0:T(8,128)(2,1)}, u32[]{:S(2)}, u32[]{:S(2)}) collective-permute-start(bf16[64,3072]{1,0:T(8,128)(2,1)S(1)} %pad_maximum_fusion.refs_4_), channel_id=1, source_target_pairs={{0,8},{4,12},{8,0},{12,4},{16,24},{20,28},{24,16},{28,20},{32,40},... | collective-permute-start | bytes 1179656 | tf_op jit(solution)/shard_map/ppermute | solution.py:312
  5.2 15.7 %collective-permute-start.4 = (bf16[64,3072]{1,0:T(8,128)(2,1)S(1)}, bf16[64,3072]{1,0:T(8,128)(2,1)}, u32[]{:S(2)}, u32[]{:S(2)}) collective-permute-start(bf16[64,3072]{1,0:T(8,128)(2,1)S(1)} %pad_maximum_fusion.refs_4_), channel_id=1, source_target_pairs={{0,4},{4,0},{8,12},{12,8},{16,20},{20,16},{24,28},{28,24},{32,36},... | collective-permute-start | bytes 1179656 | tf_op jit(solution)/shard_map/ppermute | solution.py:312
  13.8 7.2 %copy-start.5 = (bf16[64,1024]{1,0:T(8,128)(2,1)S(1)}, bf16[64,1024]{1,0:T(8,128)(2,1)}, u32[]{:S(2)}) copy-start(bf16[64,1024]{1,0:T(8,128)(2,1)} %get-tuple-element.50) | copy-start | bytes 393220
  13.8 8.8 %copy-start.4 = (bf16[64,1024]{1,0:T(8,128)(2,1)S(1)}, bf16[64,1024]{1,0:T(8,128)(2,1)}, u32[]{:S(2)}) copy-start(bf16[64,1024]{1,0:T(8,128)(2,1)} %get-tuple-element.51) | copy-start | bytes 393220
  13.8 11.7 %copy-start.3 = (bf16[64,1024]{1,0:T(8,128)(2,1)S(1)}, bf16[64,1024]{1,0:T(8,128)(2,1)}, u32[]{:S(2)}) copy-start(bf16[64,1024]{1,0:T(8,128)(2,1)} %get-tuple-element.52) | copy-start | bytes 393220
  13.8 19.8 %copy-start.1 = (s32[32]{0:T(128)S(1)}, s32[32]{0:T(128)}, u32[]{:S(2)}) copy-start(s32[32]{0:T(128)} %refs_1_.1) | copy-start | bytes 388
  13.8 19.8 %copy-start.2 = (s32[128]{0:T(128)S(1)}, s32[128]{0:T(128)}, u32[]{:S(2)}) copy-start(s32[128]{0:T(128)} %param.18) | copy-start | bytes 1540
  13.8 21.5 %copy-start = (bf16[64,1024]{1,0:T(8,128)(2,1)S(1)}, bf16[64,1024]{1,0:T(8,128)(2,1)}, u32[]{:S(2)}) copy-start(bf16[64,1024]{1,0:T(8,128)(2,1)} %get-tuple-element.54.refs_0_) | copy-start | bytes 393220
  15.9 5.0 %collective-permute-start.2 = (bf16[64,3072]{1,0:T(8,128)(2,1)}, bf16[64,3072]{1,0:T(8,128)(2,1)S(1)}, u32[]{:S(2)}, u32[]{:S(2)}) collective-permute-start(bf16[64,3072]{1,0:T(8,128)(2,1)} %collective-permute-done.refs_6_), channel_id=1, source_target_pairs={{0,4},{4,0},{8,12},{12,8},{16,20},{20,16},{24,28},{28,24},{32,36},... | collective-permute-start | bytes 1179656 | tf_op jit(solution)/shard_map/ppermute | solution.py:312
  15.9 5.0 %collective-permute-start.3 = (bf16[64,3072]{1,0:T(8,128)(2,1)S(1)}, bf16[64,3072]{1,0:T(8,128)(2,1)S(1)}, u32[]{:S(2)}, u32[]{:S(2)}) collective-permute-start(bf16[64,3072]{1,0:T(8,128)(2,1)S(1)} %collective-permute-done.1.refs_10_), channel_id=1, source_target_pairs={{0,4},{4,0},{8,12},{12,8},{16,20},{20,16},{24,28},{28,24},{32,36},... | collective-permute-start | bytes 1179656 | tf_op jit(solution)/shard_map/ppermute | solution.py:312
  16.4 12.5 %collective-permute-start.8 = (bf16[64,3072]{1,0:T(8,128)(2,1)S(1)}, bf16[64,3072]{1,0:T(8,128)(2,1)S(1)}, u32[]{:S(2)}, u32[]{:S(2)}) collective-permute-start(bf16[64,3072]{1,0:T(8,128)(2,1)S(1)} %pad_maximum_fusion.refs_4_), channel_id=1, source_target_pairs={{0,16},{4,20},{8,24},{12,28},{16,0},{20,4},{24,8},{28,12},{32,48},... | collective-permute-start | bytes 1179656 | tf_op jit(solution)/shard_map/ppermute | solution.py:312
  16.6 24.6 %all-to-all-start = ((bf16[4,128,1024]{2,1,0:T(8,128)(2,1)}), bf16[4,128,1024]{2,1,0:T(8,128)(2,1)}, u32[]{:S(2)}, u32[]{:S(2)}) async-start(bf16[4,128,1024]{2,1,0:T(8,128)(2,1)} %get-tuple-element.62), calls=%async_computation | async-start | bytes 2097152 | tf_op jit(solution)/shard_map/all_to_all | solution.py:362
  20.9 8.0 %collective-permute-start.5 = (bf16[64,1024]{1,0:T(8,128)(2,1)S(1)}, bf16[64,1024]{1,0:T(8,128)(2,1)S(1)}, u32[]{:S(2)}, u32[]{:S(2)}) collective-permute-start(bf16[64,1024]{1,0:T(8,128)(2,1)S(1)} %copy-done.5), channel_id=1, source_target_pairs={{0,32},{4,36},{8,40},{12,44},{16,48},{20,52},{24,56},{28,60},{32,0... | collective-permute-start | bytes 393224 | tf_op jit(solution)/shard_map/ppermute | solution.py:312
  22.6 8.9 %collective-permute-start.6 = (bf16[64,1024]{1,0:T(8,128)(2,1)S(1)}, bf16[64,1024]{1,0:T(8,128)(2,1)S(1)}, u32[]{:S(2)}, u32[]{:S(2)}) collective-permute-start(bf16[64,1024]{1,0:T(8,128)(2,1)S(1)} %copy-done.4), channel_id=1, source_target_pairs={{0,64},{4,68},{8,72},{12,76},{16,80},{20,84},{24,88},{28,92},{32,9... | collective-permute-start | bytes 393224 | tf_op jit(solution)/shard_map/ppermute | solution.py:312
  25.5 8.1 %collective-permute-start.7 = (bf16[64,1024]{1,0:T(8,128)(2,1)S(1)}, bf16[64,1024]{1,0:T(8,128)(2,1)S(1)}, u32[]{:S(2)}, u32[]{:S(2)}) collective-permute-start(bf16[64,1024]{1,0:T(8,128)(2,1)S(1)} %copy-done.3), channel_id=1, source_target_pairs={{0,96},{4,100},{8,104},{12,108},{16,112},{20,116},{24,120},{28,124... | collective-permute-start | bytes 393224 | tf_op jit(solution)/shard_map/ppermute | solution.py:312
  33.6 1.7 %collective-permute-start.9 = (bf16[64,3072]{1,0:T(8,128)(2,1)S(1)}, bf16[64,3072]{1,0:T(8,128)(2,1)S(1)}, u32[]{:S(2)}, u32[]{:S(2)}) collective-permute-start(bf16[64,3072]{1,0:T(8,128)(2,1)S(1)} %collective-permute-done.8.refs_8_), channel_id=1, source_target_pairs={{0,4},{4,0},{8,12},{12,8},{16,20},{20,16},{24,28},{28,24},{32,36},... | collective-permute-start | bytes 1179656 | tf_op jit(solution)/shard_map/ppermute | solution.py:312
  36.9 5.5 %collective-permute-start.12 = (f32[128,128]{1,0:T(8,128)S(1)}, f32[128,128]{1,0:T(8,128)S(1)}, u32[]{:S(2)}, u32[]{:S(2)}) collective-permute-start(f32[128,128]{1,0:T(8,128)S(1)} %shard_map.110.refs_0_), channel_id=1, source_target_pairs={{0,3},{1,2},{2,1},{3,0},{4,7},{5,6},{6,5},{7,4},{8,11},{9,10},{10,... | collective-permute-start | bytes 196616 | tf_op jit(solution)/shard_map/ppermute | solution.py:308
  39.6 6.1 %collective-permute-start.11 = (f32[128,128]{1,0:T(8,128)S(1)}, f32[128,128]{1,0:T(8,128)S(1)}, u32[]{:S(2)}, u32[]{:S(2)}) collective-permute-start(f32[128,128]{1,0:T(8,128)S(1)} %shard_map.110.refs_0_), channel_id=1, source_target_pairs={{0,2},{1,3},{2,0},{3,1},{4,6},{5,7},{6,4},{7,5},{8,10},{9,11},{10,... | collective-permute-start | bytes 196616 | tf_op jit(solution)/shard_map/ppermute | solution.py:308
  40.5 5.2 %collective-permute-start.10 = (f32[128,128]{1,0:T(8,128)S(1)}, f32[128,128]{1,0:T(8,128)S(1)}, u32[]{:S(2)}, u32[]{:S(2)}) collective-permute-start(f32[128,128]{1,0:T(8,128)S(1)} %shard_map.110.refs_0_), channel_id=1, source_target_pairs={{0,1},{1,0},{2,3},{3,2},{4,5},{5,4},{6,7},{7,6},{8,9},{9,8},{10,11... | collective-permute-start | bytes 196616 | tf_op jit(solution)/shard_map/ppermute | solution.py:308
  47.6 12.1 %collective-permute-start.13 = (bf16[64,2048]{1,0:T(8,128)(2,1)S(1)}, bf16[64,2048]{1,0:T(8,128)(2,1)S(1)}, u32[]{:S(2)}, u32[]{:S(2)}) collective-permute-start(bf16[64,2048]{1,0:T(8,128)(2,1)S(1)} %get-tuple-element.70), channel_id=1, source_target_pairs={{0,32},{4,36},{8,40},{12,44},{16,48},{20,52},{24,56},{28,60},{32,0... | collective-permute-start | bytes 786440 | tf_op jit(solution)/shard_map/ppermute | solution.py:312
  47.7 12.6 %collective-permute-start.14 = (bf16[64,2048]{1,0:T(8,128)(2,1)S(1)}, bf16[64,2048]{1,0:T(8,128)(2,1)S(1)}, u32[]{:S(2)}, u32[]{:S(2)}) collective-permute-start(bf16[64,2048]{1,0:T(8,128)(2,1)S(1)} %get-tuple-element.71), channel_id=1, source_target_pairs={{0,64},{4,68},{8,72},{12,76},{16,80},{20,84},{24,88},{28,92},{32,9... | collective-permute-start | bytes 786440 | tf_op jit(solution)/shard_map/ppermute | solution.py:312
  49.9 12.9 %collective-permute-start.15 = (bf16[64,2048]{1,0:T(8,128)(2,1)S(1)}, bf16[64,2048]{1,0:T(8,128)(2,1)S(1)}, u32[]{:S(2)}, u32[]{:S(2)}) collective-permute-start(bf16[64,2048]{1,0:T(8,128)(2,1)S(1)} %get-tuple-element.72), channel_id=1, source_target_pairs={{0,96},{4,100},{8,104},{12,108},{16,112},{20,116},{24,120},{28,124... | collective-permute-start | bytes 786440 | tf_op jit(solution)/shard_map/ppermute | solution.py:312

commit v4 on v3

--- a/solution.py
+++ b/solution.py
@@ -360,14 +360,12 @@
         owned * CAP,
     )
     pieces = lax.all_to_all(attended, "tensor", 0, 0)
-    placed, beside, both_late, request_adapter = lax.optimization_barrier(
-        (placed, beside, both, request_adapter)
+    placed, both_late, request_adapter = lax.optimization_barrier(
+        (placed, both, request_adapter)
     )
     across = swap_z(both_late, 2)
+    placed, beside, both_other = lax.optimization_barrier((placed, beside, both_other))
     beside_other = [swap_core(w) for w in beside]
-    placed, beside_other, both_other = lax.optimization_barrier(
-        (placed, beside_other, both_other)
-    )
     routed = [placed[0]] + [swap_y(placed[m], m) for m in range(1, RING)]
     routed, across = lax.optimization_barrier((routed, across))
     table = [both, both_other, beside[0], beside_other[0]]

time: 64.3 us -> 63.2 us (0.983)
  waiting for transfers between devices: 19.2 us -> 17.1 us
  starting transfers between devices: 22.9 us -> 23.9 us
    ppermute x13, waiting for transfers between devices: 14.7 us -> 12.6 us  [swap_dp(): lax.ppermute(value, 'dp', [(i, i ^ k) for i in range(RING * Z_CHIPS * COR...]
    ppermute x13, starting transfers between devices: 14.5 us -> 15.5 us  [swap_dp(): lax.ppermute(value, 'dp', [(i, i ^ k) for i in range(RING * Z_CHIPS * COR...]
  transfers between devices with their start and end apart: 17 -> 17, of which waited for: 10 -> 8; matrix products, arithmetic and copies ran while one was open for 0% -> 0% of each run, Pallas kernels for 27% -> 28%
where the time goes in v4:
time: 63.2 us; the launch traced here: 63 us
  starting transfers between devices  23.9 us (38%)
  Pallas kernels  19.3 us (31%)
  waiting for transfers between devices  17.1 us (27%)
  other arithmetic  2.17 us (3%)
    ppermute x13, starting transfers between devices, swap_dp(): lax.ppermute(value, 'dp', [(i, i ^ k) for i in range(RING * Z_CHIPS * COR...  15.5 us
    ppermute x13, waiting for transfers between devices, swap_dp(): lax.ppermute(value, 'dp', [(i, i ^ k) for i in range(RING * Z_CHIPS * COR...  12.6 us
    pallas_call x1, Pallas kernels, attend(): pl.pallas_call(attend_kernel, in_specs=[hbm] * (STAGED + 2), out_specs=[v...  8.55 us
    pallas_call x1, Pallas kernels, project(): pl.pallas_call(project_kernel, in_specs=[hbm, hbm], out_specs=pl.BlockSpe...  7.27 us
    ppermute x3, waiting for transfers between devices, swap_tensor(): return lax.ppermute(value, 'tensor', [(i, i ^ k) for i in range(RING)])  4.49 us
    all_to_all x1, starting transfers between devices, on_device(): pieces = lax.all_to_all(attended, 'tensor', 0, 0)  4.29 us
    ppermute x3, starting transfers between devices, swap_tensor(): return lax.ppermute(value, 'tensor', [(i, i ^ k) for i in range(RING)])  4.12 us
    pallas_call x1, Pallas kernels, up(): pl.pallas_call(functools.partial(up_kernel, columns), in_specs=[vmem] * (...  1.88 us
  transfers between devices with their start and end apart: 17, of which 8 were waited for; matrix products, arithmetic and copies ran while one was open for 0% of the time, Pallas kernels for 28%

profile of v4, /device:TPU:0, one launch (start us, length us, event | category | flops | bytes accessed | tf_op | source)
XLA Modules:
  0.0 63.0 jit_solution(16829530826471974013)
XLA Ops:
  0.0 1.0 %pad_maximum_fusion.refs_4_ = bf16[64,3072]{1,0:T(8,128)(2,1)S(1)} fusion(bf16[64,2048]{1,0:T(8,128)(2,1)} %bitcast.3, bf16[64,1024]{1,0:T(8,128)(2,1)} %bitcast.4), kind=kLoop, calls=%fused_computation.9 | loop fusion | flops 786432 | bytes 786432 | tf_op jit(solution)/shard_map/concatenate | solution.py:347
  1.1 4.2 %collective-permute-start.1 = (bf16[64,3072]{1,0:T(8,128)(2,1)S(1)}, bf16[64,3072]{1,0:T(8,128)(2,1)}, u32[]{:S(2)}, u32[]{:S(2)}) collective-permute-start(bf16[64,3072]{1,0:T(8,128)(2,1)S(1)} %pad_maximum_fusion.refs_4_), channel_id=1, source_target_pairs={{0,24},{4,28},{8,16},{12,20},{16,8},{20,12},{24,0},{28,4},{32,56},... | collective-permute-start | bytes 1179656 | tf_op jit(solution)/shard_map/ppermute | solution.py:312
  5.3 8.6 %shard_map.109 = (bf16[4,128,1024]{2,1,0:T(8,128)(2,1)}, bf16[64,1024]{1,0:T(8,128)(2,1)}, bf16[64,1024]{1,0:T(8,128)(2,1)}, bf16[64,1024]{1,0:T(8,128)(2,1)}, bf16[64,1024]{1,0:T(8,128)(2,1)}) custom-call(s32[128]{0:T(128)} %refs_0_.1, s32[32]{0:T(128)} %refs_1_.1, s32[1,128]{1,0:T(1,128)} %bitcast.5, bf16[128,1024]{1,0:T(8,128)(2,1)} %refs_3_.1, ...), custom_call_target="tpu_custom_call" | custom-call | flops 134217728 | bytes 16777216 | tf_op jit(solution)/shard_map/pallas_call | solution.py:144
  13.9 1.6 %collective-permute-start.6 = (bf16[64,3072]{1,0:T(8,128)(2,1)S(1)}, bf16[64,3072]{1,0:T(8,128)(2,1)S(1)}, u32[]{:S(2)}, u32[]{:S(2)}) collective-permute-start(bf16[64,3072]{1,0:T(8,128)(2,1)S(1)} %pad_maximum_fusion.refs_4_), channel_id=1, source_target_pairs={{0,16},{4,20},{8,24},{12,28},{16,0},{20,4},{24,8},{28,12},{32,48},... | collective-permute-start | bytes 1179656 | tf_op jit(solution)/shard_map/ppermute | solution.py:312
  15.6 4.3 %all-to-all-start = ((bf16[4,128,1024]{2,1,0:T(8,128)(2,1)}), bf16[4,128,1024]{2,1,0:T(8,128)(2,1)}, u32[]{:S(2)}, u32[]{:S(2)}) async-start(bf16[4,128,1024]{2,1,0:T(8,128)(2,1)} %get-tuple-element.58), calls=%async_computation | async-start | bytes 2097152 | tf_op jit(solution)/shard_map/all_to_all | solution.py:362
  19.9 1.7 %collective-permute-start.3 = (bf16[64,1024]{1,0:T(8,128)(2,1)S(1)}, bf16[64,1024]{1,0:T(8,128)(2,1)S(1)}, u32[]{:S(2)}, u32[]{:S(2)}) collective-permute-start(bf16[64,1024]{1,0:T(8,128)(2,1)S(1)} %copy-done.5), channel_id=1, source_target_pairs={{0,32},{4,36},{8,40},{12,44},{16,48},{20,52},{24,56},{28,60},{32,0... | collective-permute-start | bytes 393224 | tf_op jit(solution)/shard_map/ppermute | solution.py:312
  21.5 2.9 %collective-permute-start.4 = (bf16[64,1024]{1,0:T(8,128)(2,1)S(1)}, bf16[64,1024]{1,0:T(8,128)(2,1)S(1)}, u32[]{:S(2)}, u32[]{:S(2)}) collective-permute-start(bf16[64,1024]{1,0:T(8,128)(2,1)S(1)} %copy-done.4), channel_id=1, source_target_pairs={{0,64},{4,68},{8,72},{12,76},{16,80},{20,84},{24,88},{28,92},{32,9... | collective-permute-start | bytes 393224 | tf_op jit(solution)/shard_map/ppermute | solution.py:312
  24.7 2.0 %collective-permute-done.6.refs_8_ = bf16[64,3072]{1,0:T(8,128)(2,1)S(1)} collective-permute-done((bf16[64,3072]{1,0:T(8,128)(2,1)S(1)}, bf16[64,3072]{1,0:T(8,128)(2,1)S(1)}, u32[]{:S(2)}, u32[]{:S(2)}) %collective-permute-start.6) | collective-permute-done | bytes 393248 | tf_op jit(solution)/shard_map/ppermute | solution.py:312
  26.7 3.8 %collective-permute-done.4.refs_2_ = bf16[64,1024]{1,0:T(8,128)(2,1)S(1)} collective-permute-done((bf16[64,1024]{1,0:T(8,128)(2,1)S(1)}, bf16[64,1024]{1,0:T(8,128)(2,1)S(1)}, u32[]{:S(2)}, u32[]{:S(2)}) %collective-permute-start.4) | collective-permute-done | bytes 131104 | tf_op jit(solution)/shard_map/ppermute | solution.py:312
  30.5 2.0 %collective-permute-done.5.refs_3_ = bf16[64,1024]{1,0:T(8,128)(2,1)S(1)} collective-permute-done((bf16[64,1024]{1,0:T(8,128)(2,1)S(1)}, bf16[64,1024]{1,0:T(8,128)(2,1)S(1)}, u32[]{:S(2)}, u32[]{:S(2)}) %collective-permute-start.5) | collective-permute-done | bytes 131104 | tf_op jit(solution)/shard_map/ppermute | solution.py:312
  32.6 1.6 %collective-permute-done.8.refs_9_ = bf16[64,3072]{1,0:T(8,128)(2,1)S(1)} collective-permute-done((bf16[64,3072]{1,0:T(8,128)(2,1)S(1)}, bf16[64,3072]{1,0:T(8,128)(2,1)S(1)}, u32[]{:S(2)}, u32[]{:S(2)}) %collective-permute-start.8) | collective-permute-done | bytes 393248 | tf_op jit(solution)/shard_map/ppermute | solution.py:312
  34.2 1.6 %shard_map.110.refs_0_ = f32[128,128]{1,0:T(8,128)S(1)} custom-call(bf16[64,1024]{1,0:T(8,128)(2,1)S(1)} %copy-done, bf16[64,1024]{1,0:T(8,128)(2,1)S(1)} %collective-permute-done.3.refs_1_, bf16[64,1024]{1,0:T(8,128)(2,1)S(1)} %collective-permute-done.4.refs_2_, bf16[64,1024]{1,0:T(8,128)(2,1)S(1)} %collective-permute-done.5.refs_3_, ...), custom_call_target="tpu_custom_call" | custom-call | tf_op jit(solution)/shard_map/pallas_call | solution.py:205
  35.8 2.7 %collective-permute-start.12 = (f32[128,128]{1,0:T(8,128)S(1)}, f32[128,128]{1,0:T(8,128)S(1)}, u32[]{:S(2)}, u32[]{:S(2)}) collective-permute-start(f32[128,128]{1,0:T(8,128)S(1)} %shard_map.110.refs_0_), channel_id=1, source_target_pairs={{0,3},{1,2},{2,1},{3,0},{4,7},{5,6},{6,5},{7,4},{8,11},{9,10},{10,... | collective-permute-start | bytes 196616 | tf_op jit(solution)/shard_map/ppermute | solution.py:308
  38.5 0.9 %collective-permute-start.11 = (f32[128,128]{1,0:T(8,128)S(1)}, f32[128,128]{1,0:T(8,128)S(1)}, u32[]{:S(2)}, u32[]{:S(2)}) collective-permute-start(f32[128,128]{1,0:T(8,128)S(1)} %shard_map.110.refs_0_), channel_id=1, source_target_pairs={{0,2},{1,3},{2,0},{3,1},{4,6},{5,7},{6,4},{7,5},{8,10},{9,11},{10,... | collective-permute-start | bytes 196616 | tf_op jit(solution)/shard_map/ppermute | solution.py:308
  39.4 0.5 collective-permute-start.10
  40.1 1.2 %collective-permute-done.12.refs_3_ = f32[128,128]{1,0:T(8,128)S(1)} collective-permute-done((f32[128,128]{1,0:T(8,128)S(1)}, f32[128,128]{1,0:T(8,128)S(1)}, u32[]{:S(2)}, u32[]{:S(2)}) %collective-permute-start.12) | collective-permute-done | bytes 65568 | tf_op jit(solution)/shard_map/ppermute | solution.py:308
  41.3 3.3 %collective-permute-done.11.refs_2_ = f32[128,128]{1,0:T(8,128)S(1)} collective-permute-done((f32[128,128]{1,0:T(8,128)S(1)}, f32[128,128]{1,0:T(8,128)S(1)}, u32[]{:S(2)}, u32[]{:S(2)}) %collective-permute-start.11) | collective-permute-done | bytes 65568 | tf_op jit(solution)/shard_map/ppermute | solution.py:308
  44.6 1.9 %shard_map.112 = (bf16[64,2048]{1,0:T(8,128)(2,1)S(1)}, bf16[64,2048]{1,0:T(8,128)(2,1)S(1)}, bf16[64,2048]{1,0:T(8,128)(2,1)S(1)}, bf16[64,2048]{1,0:T(8,128)(2,1)S(1)}) custom-call(f32[128,128]{1,0:T(8,128)S(1)} %shard_map.110.refs_0_, f32[128,128]{1,0:T(8,128)S(1)} %collective-permute-done.10.refs_1_, f32[128,128]{1,0:T(8,128)S(1)} %collective-permute-done.11.refs_2_, ...), custom_call_target="tpu_custom_call" | custom-call | tf_op jit(solution)/shard_map/pallas_call | solution.py:244
  46.6 2.2 %collective-permute-start.14 = (bf16[64,2048]{1,0:T(8,128)(2,1)S(1)}, bf16[64,2048]{1,0:T(8,128)(2,1)S(1)}, u32[]{:S(2)}, u32[]{:S(2)}) collective-permute-start(bf16[64,2048]{1,0:T(8,128)(2,1)S(1)} %get-tuple-element.67), channel_id=1, source_target_pairs={{0,64},{4,68},{8,72},{12,76},{16,80},{20,84},{24,88},{28,92},{32,9... | collective-permute-start | bytes 786440 | tf_op jit(solution)/shard_map/ppermute | solution.py:312
  48.8 2.4 %collective-permute-start.15 = (bf16[64,2048]{1,0:T(8,128)(2,1)S(1)}, bf16[64,2048]{1,0:T(8,128)(2,1)S(1)}, u32[]{:S(2)}, u32[]{:S(2)}) collective-permute-start(bf16[64,2048]{1,0:T(8,128)(2,1)S(1)} %get-tuple-element.68), channel_id=1, source_target_pairs={{0,96},{4,100},{8,104},{12,108},{16,112},{20,116},{24,120},{28,124... | collective-permute-start | bytes 786440 | tf_op jit(solution)/shard_map/ppermute | solution.py:312
  51.3 7.3 %shard_map.111 = f32[128,2048]{1,0:T(8,128)S(1)} custom-call(bf16[4,128,1024]{2,1,0:T(8,128)(2,1)} %all-to-all-done.piece_hbm, bf16[4096,2048]{1,0:T(8,128)(2,1)} %weight_hbm.1), custom_call_target="tpu_custom_call" | custom-call | flops 2147483648 | bytes 16777216 | tf_op jit(solution)/shard_map/pallas_call | solution.py:287
  58.6 0.6 collective-permute-done.14
  59.2 2.6 %collective-permute-done.15 = bf16[64,2048]{1,0:T(8,128)(2,1)S(1)} collective-permute-done((bf16[64,2048]{1,0:T(8,128)(2,1)S(1)}, bf16[64,2048]{1,0:T(8,128)(2,1)S(1)}, u32[]{:S(2)}, u32[]{:S(2)}) %collective-permute-start.15) | collective-permute-done | bytes 262176 | tf_op jit(solution)/shard_map/ppermute | solution.py:312
  62.1 0.9 %add_convert_fusion = bf16[128,2048]{1,0:T(8,128)(2,1)} fusion(f32[128,2048]{1,0:T(8,128)S(1)} %shard_map.111, f32[128,2048]{1,0:T(8,128)S(1)} %fusion), kind=kLoop, calls=%fused_computation.8 | loop fusion | flops 524288 | bytes 2621440 | tf_op jit(solution)/shard_map/convert_element_type | solution.py:392
  (32 shorter events, 1.1 us)
Async XLA Ops:
  1.0 18.9 %collective-permute-start.2 = (bf16[64,3072]{1,0:T(8,128)(2,1)S(1)}, bf16[64,3072]{1,0:T(8,128)(2,1)S(1)}, u32[]{:S(2)}, u32[]{:S(2)}) collective-permute-start(bf16[64,3072]{1,0:T(8,128)(2,1)S(1)} %pad_maximum_fusion.refs_4_), channel_id=1, source_target_pairs={{0,4},{4,0},{8,12},{12,8},{16,20},{20,16},{24,28},{28,24},{32,36},... | collective-permute-start | bytes 1179656 | tf_op jit(solution)/shard_map/ppermute | solution.py:312
  1.1 18.8 %collective-permute-start.1 = (bf16[64,3072]{1,0:T(8,128)(2,1)S(1)}, bf16[64,3072]{1,0:T(8,128)(2,1)}, u32[]{:S(2)}, u32[]{:S(2)}) collective-permute-start(bf16[64,3072]{1,0:T(8,128)(2,1)S(1)} %pad_maximum_fusion.refs_4_), channel_id=1, source_target_pairs={{0,24},{4,28},{8,16},{12,20},{16,8},{20,12},{24,0},{28,4},{32,56},... | collective-permute-start | bytes 1179656 | tf_op jit(solution)/shard_map/ppermute | solution.py:312
  5.3 14.6 %collective-permute-start = (bf16[64,3072]{1,0:T(8,128)(2,1)S(1)}, bf16[64,3072]{1,0:T(8,128)(2,1)}, u32[]{:S(2)}, u32[]{:S(2)}) collective-permute-start(bf16[64,3072]{1,0:T(8,128)(2,1)S(1)} %pad_maximum_fusion.refs_4_), channel_id=1, source_target_pairs={{0,8},{4,12},{8,0},{12,4},{16,24},{20,28},{24,16},{28,20},{32,40},... | collective-permute-start | bytes 1179656 | tf_op jit(solution)/shard_map/ppermute | solution.py:312
  13.9 6.0 %copy-start.5 = (bf16[64,1024]{1,0:T(8,128)(2,1)S(1)}, bf16[64,1024]{1,0:T(8,128)(2,1)}, u32[]{:S(2)}) copy-start(bf16[64,1024]{1,0:T(8,128)(2,1)} %get-tuple-element.46) | copy-start | bytes 393220
  13.9 7.7 %copy-start.4 = (bf16[64,1024]{1,0:T(8,128)(2,1)S(1)}, bf16[64,1024]{1,0:T(8,128)(2,1)}, u32[]{:S(2)}) copy-start(bf16[64,1024]{1,0:T(8,128)(2,1)} %get-tuple-element.47) | copy-start | bytes 393220
  13.9 10.6 %copy-start.3 = (bf16[64,1024]{1,0:T(8,128)(2,1)S(1)}, bf16[64,1024]{1,0:T(8,128)(2,1)}, u32[]{:S(2)}) copy-start(bf16[64,1024]{1,0:T(8,128)(2,1)} %get-tuple-element.48) | copy-start | bytes 393220
  13.9 18.6 %copy-start.1 = (s32[32]{0:T(128)S(1)}, s32[32]{0:T(128)}, u32[]{:S(2)}) copy-start(s32[32]{0:T(128)} %refs_1_.1) | copy-start | bytes 388
  13.9 18.6 %copy-start.2 = (s32[128]{0:T(128)S(1)}, s32[128]{0:T(128)}, u32[]{:S(2)}) copy-start(s32[128]{0:T(128)} %param.18) | copy-start | bytes 1540
  13.9 20.3 %copy-start = (bf16[64,1024]{1,0:T(8,128)(2,1)S(1)}, bf16[64,1024]{1,0:T(8,128)(2,1)}, u32[]{:S(2)}) copy-start(bf16[64,1024]{1,0:T(8,128)(2,1)} %get-tuple-element.50.refs_0_) | copy-start | bytes 393220
  13.9 12.8 %collective-permute-start.6 = (bf16[64,3072]{1,0:T(8,128)(2,1)S(1)}, bf16[64,3072]{1,0:T(8,128)(2,1)S(1)}, u32[]{:S(2)}, u32[]{:S(2)}) collective-permute-start(bf16[64,3072]{1,0:T(8,128)(2,1)S(1)} %pad_maximum_fusion.refs_4_), channel_id=1, source_target_pairs={{0,16},{4,20},{8,24},{12,28},{16,0},{20,4},{24,8},{28,12},{32,48},... | collective-permute-start | bytes 1179656 | tf_op jit(solution)/shard_map/ppermute | solution.py:312
  15.6 24.5 %all-to-all-start = ((bf16[4,128,1024]{2,1,0:T(8,128)(2,1)}), bf16[4,128,1024]{2,1,0:T(8,128)(2,1)}, u32[]{:S(2)}, u32[]{:S(2)}) async-start(bf16[4,128,1024]{2,1,0:T(8,128)(2,1)} %get-tuple-element.58), calls=%async_computation | async-start | bytes 2097152 | tf_op jit(solution)/shard_map/all_to_all | solution.py:362
  19.9 6.8 %collective-permute-start.3 = (bf16[64,1024]{1,0:T(8,128)(2,1)S(1)}, bf16[64,1024]{1,0:T(8,128)(2,1)S(1)}, u32[]{:S(2)}, u32[]{:S(2)}) collective-permute-start(bf16[64,1024]{1,0:T(8,128)(2,1)S(1)} %copy-done.5), channel_id=1, source_target_pairs={{0,32},{4,36},{8,40},{12,44},{16,48},{20,52},{24,56},{28,60},{32,0... | collective-permute-start | bytes 393224 | tf_op jit(solution)/shard_map/ppermute | solution.py:312
  21.5 8.9 %collective-permute-start.4 = (bf16[64,1024]{1,0:T(8,128)(2,1)S(1)}, bf16[64,1024]{1,0:T(8,128)(2,1)S(1)}, u32[]{:S(2)}, u32[]{:S(2)}) collective-permute-start(bf16[64,1024]{1,0:T(8,128)(2,1)S(1)} %copy-done.4), channel_id=1, source_target_pairs={{0,64},{4,68},{8,72},{12,76},{16,80},{20,84},{24,88},{28,92},{32,9... | collective-permute-start | bytes 393224 | tf_op jit(solution)/shard_map/ppermute | solution.py:312
  24.5 8.0 %collective-permute-start.5 = (bf16[64,1024]{1,0:T(8,128)(2,1)S(1)}, bf16[64,1024]{1,0:T(8,128)(2,1)S(1)}, u32[]{:S(2)}, u32[]{:S(2)}) collective-permute-start(bf16[64,1024]{1,0:T(8,128)(2,1)S(1)} %copy-done.3), channel_id=1, source_target_pairs={{0,96},{4,100},{8,104},{12,108},{16,112},{20,116},{24,120},{28,124... | collective-permute-start | bytes 393224 | tf_op jit(solution)/shard_map/ppermute | solution.py:312
  24.7 7.9 %collective-permute-start.7 = (bf16[64,3072]{1,0:T(8,128)(2,1)}, bf16[64,3072]{1,0:T(8,128)(2,1)S(1)}, u32[]{:S(2)}, u32[]{:S(2)}) collective-permute-start(bf16[64,3072]{1,0:T(8,128)(2,1)} %collective-permute-done.refs_6_), channel_id=1, source_target_pairs={{0,4},{4,0},{8,12},{12,8},{16,20},{20,16},{24,28},{28,24},{32,36},... | collective-permute-start | bytes 1179656 | tf_op jit(solution)/shard_map/ppermute | solution.py:312
  26.7 5.9 %collective-permute-start.9 = (bf16[64,3072]{1,0:T(8,128)(2,1)}, bf16[64,3072]{1,0:T(8,128)(2,1)S(1)}, u32[]{:S(2)}, u32[]{:S(2)}) collective-permute-start(bf16[64,3072]{1,0:T(8,128)(2,1)} %collective-permute-done.1.refs_10_), channel_id=1, source_target_pairs={{0,4},{4,0},{8,12},{12,8},{16,20},{20,16},{24,28},{28,24},{32,36},... | collective-permute-start | bytes 1179656 | tf_op jit(solution)/shard_map/ppermute | solution.py:312
  32.5 1.7 %collective-permute-start.8 = (bf16[64,3072]{1,0:T(8,128)(2,1)S(1)}, bf16[64,3072]{1,0:T(8,128)(2,1)S(1)}, u32[]{:S(2)}, u32[]{:S(2)}) collective-permute-start(bf16[64,3072]{1,0:T(8,128)(2,1)S(1)} %collective-permute-done.6.refs_8_), channel_id=1, source_target_pairs={{0,4},{4,0},{8,12},{12,8},{16,20},{20,16},{24,28},{28,24},{32,36},... | collective-permute-start | bytes 1179656 | tf_op jit(solution)/shard_map/ppermute | solution.py:312
  35.8 5.5 %collective-permute-start.12 = (f32[128,128]{1,0:T(8,128)S(1)}, f32[128,128]{1,0:T(8,128)S(1)}, u32[]{:S(2)}, u32[]{:S(2)}) collective-permute-start(f32[128,128]{1,0:T(8,128)S(1)} %shard_map.110.refs_0_), channel_id=1, source_target_pairs={{0,3},{1,2},{2,1},{3,0},{4,7},{5,6},{6,5},{7,4},{8,11},{9,10},{10,... | collective-permute-start | bytes 196616 | tf_op jit(solution)/shard_map/ppermute | solution.py:308
  38.5 6.1 %collective-permute-start.11 = (f32[128,128]{1,0:T(8,128)S(1)}, f32[128,128]{1,0:T(8,128)S(1)}, u32[]{:S(2)}, u32[]{:S(2)}) collective-permute-start(f32[128,128]{1,0:T(8,128)S(1)} %shard_map.110.refs_0_), channel_id=1, source_target_pairs={{0,2},{1,3},{2,0},{3,1},{4,6},{5,7},{6,4},{7,5},{8,10},{9,11},{10,... | collective-permute-start | bytes 196616 | tf_op jit(solution)/shard_map/ppermute | solution.py:308
  39.4 5.2 %collective-permute-start.10 = (f32[128,128]{1,0:T(8,128)S(1)}, f32[128,128]{1,0:T(8,128)S(1)}, u32[]{:S(2)}, u32[]{:S(2)}) collective-permute-start(f32[128,128]{1,0:T(8,128)S(1)} %shard_map.110.refs_0_), channel_id=1, source_target_pairs={{0,1},{1,0},{2,3},{3,2},{4,5},{5,4},{6,7},{7,6},{8,9},{9,8},{10,11... | collective-permute-start | bytes 196616 | tf_op jit(solution)/shard_map/ppermute | solution.py:308
  46.5 12.1 %collective-permute-start.13 = (bf16[64,2048]{1,0:T(8,128)(2,1)S(1)}, bf16[64,2048]{1,0:T(8,128)(2,1)S(1)}, u32[]{:S(2)}, u32[]{:S(2)}) collective-permute-start(bf16[64,2048]{1,0:T(8,128)(2,1)S(1)} %get-tuple-element.66), channel_id=1, source_target_pairs={{0,32},{4,36},{8,40},{12,44},{16,48},{20,52},{24,56},{28,60},{32,0... | collective-permute-start | bytes 786440 | tf_op jit(solution)/shard_map/ppermute | solution.py:312
  46.6 12.6 %collective-permute-start.14 = (bf16[64,2048]{1,0:T(8,128)(2,1)S(1)}, bf16[64,2048]{1,0:T(8,128)(2,1)S(1)}, u32[]{:S(2)}, u32[]{:S(2)}) collective-permute-start(bf16[64,2048]{1,0:T(8,128)(2,1)S(1)} %get-tuple-element.67), channel_id=1, source_target_pairs={{0,64},{4,68},{8,72},{12,76},{16,80},{20,84},{24,88},{28,92},{32,9... | collective-permute-start | bytes 786440 | tf_op jit(solution)/shard_map/ppermute | solution.py:312
  48.8 12.9 %collective-permute-start.15 = (bf16[64,2048]{1,0:T(8,128)(2,1)S(1)}, bf16[64,2048]{1,0:T(8,128)(2,1)S(1)}, u32[]{:S(2)}, u32[]{:S(2)}) collective-permute-start(bf16[64,2048]{1,0:T(8,128)(2,1)S(1)} %get-tuple-element.68), channel_id=1, source_target_pairs={{0,96},{4,100},{8,104},{12,108},{16,112},{20,116},{24,120},{28,124... | collective-permute-start | bytes 786440 | tf_op jit(solution)/shard_map/ppermute | solution.py:312

commit v5 on v4

--- a/solution.py
+++ b/solution.py
@@ -16,7 +16,7 @@
 CORES = 2
 RING = 4
 GROUP = HEADS // KV_HEADS
-BLOCK = 32
+BLOCKS = (16, 32, 32, 32, 16)
 ATTEND_VMEM = 63 * 2**20
 STAGED = 6
 AHEAD = 2
@@ -47,11 +47,11 @@
     key_ref, value_ref, heads_ref, mixed_ref, staged_sem, key_sem, value_sem = refs
     f32, bf16 = jnp.float32, jnp.bfloat16
     requests, positions, _ = key_ref.shape
-    blocks = requests // BLOCK
+    blocks = len(BLOCKS)
     score_scale = 1.0 / math.sqrt(HEAD_DIM)
 
     def fetch(source, target, sem, c):
-        at = pl.ds(c * BLOCK, BLOCK)
+        at = pl.ds(sum(BLOCKS[:c]), BLOCKS[c])
         return pltpu.make_async_copy(source.at[at], target.at[at], sem.at[c])
 
     staging = [
@@ -73,12 +73,13 @@
     for c in range(blocks):
         if c + AHEAD < blocks:
             start(c + AHEAD)
-        rows = slice(c * BLOCK, (c + 1) * BLOCK)
+        first, block = sum(BLOCKS[:c]), BLOCKS[c]
+        rows = slice(first, first + block)
         for h in range(GROUP):
-            heads_ref[pl.ds(h, BLOCK, stride=GROUP), :] = query_ref[
+            heads_ref[pl.ds(h, block, stride=GROUP), :] = query_ref[
                 rows, h * HEAD_DIM : (h + 1) * HEAD_DIM
             ].astype(f32)
-        heads = heads_ref[...].reshape(BLOCK, GROUP, HEAD_DIM)
+        heads = heads_ref[: block * GROUP, :].reshape(block, GROUP, HEAD_DIM)
         fresh_keys = token_key_ref[rows, :].astype(f32)[:, None, :]
         fresh_values = token_value_ref[rows, :].astype(f32)[:, None, :]
         fetch(key_hbm, key_ref, key_sem, c).wait()
@@ -92,8 +93,8 @@
         place = lax.broadcasted_iota(jnp.int32, (GROUP, positions), 1)
         score = jnp.stack(
             [
-                jnp.where(place < length_ref[c * BLOCK + r], score[r], -jnp.inf)
-                for r in range(BLOCK)
+                jnp.where(place < length_ref[first + r], score[r], -jnp.inf)
+                for r in range(block)
             ]
         )
         row_max = jnp.maximum(jnp.max(score, axis=2, keepdims=True), fresh)
@@ -108,10 +109,10 @@
             preferred_element_type=f32,
         )
         mixed = mixed + fresh_weight.astype(bf16).astype(f32) * fresh_values
-        mixed_ref[...] = (mixed / weight_sum).reshape(BLOCK * GROUP, HEAD_DIM)
+        mixed_ref[: block * GROUP, :] = (mixed / weight_sum).reshape(block * GROUP, HEAD_DIM)
         for h in range(GROUP):
             attended_ref[0, rows, h * HEAD_DIM : (h + 1) * HEAD_DIM] = mixed_ref[
-                pl.ds(h, BLOCK, stride=GROUP), :
+                pl.ds(h, block, stride=GROUP), :
             ].astype(bf16)
 
     attended = attended_ref[0]
@@ -139,8 +140,8 @@
     positions = cached_key_rows.shape[1]
     vmem = pl.BlockSpec(memory_space=pltpu.VMEM)
     hbm = pl.BlockSpec(memory_space=pltpu.HBM)
-    per_head = pltpu.VMEM((BLOCK * GROUP, HEAD_DIM), jnp.float32)
-    fetches = pltpu.SemaphoreType.DMA((requests // BLOCK,))
+    per_head = pltpu.VMEM((max(BLOCKS) * GROUP, HEAD_DIM), jnp.float32)
+    fetches = pltpu.SemaphoreType.DMA((len(BLOCKS),))
     return pl.pallas_call(
         attend_kernel,
         in_specs=[hbm] * (STAGED + 2),

time: 63.2 us -> 63.1 us (level)
  transfers between devices with their start and end apart: 17 -> 17, of which waited for: 8 -> 8; matrix products, arithmetic and copies ran while one was open for 0% -> 0% of each run, Pallas kernels for 28% -> 27%
where the time goes in v5:
time: 63.1 us; the launch traced here: 62.8 us
  starting transfers between devices  23.9 us (38%)
  Pallas kernels  19.1 us (30%)
  waiting for transfers between devices  17.1 us (27%)
  other arithmetic  2.17 us (3%)
    ppermute x13, starting transfers between devices, swap_dp(): lax.ppermute(value, 'dp', [(i, i ^ k) for i in range(RING * Z_CHIPS * COR...  15.5 us
    ppermute x13, waiting for transfers between devices, swap_dp(): lax.ppermute(value, 'dp', [(i, i ^ k) for i in range(RING * Z_CHIPS * COR...  12.6 us
    pallas_call x1, Pallas kernels, attend(): pl.pallas_call(attend_kernel, in_specs=[hbm] * (STAGED + 2), out_specs=[v...  8.39 us
    pallas_call x1, Pallas kernels, project(): pl.pallas_call(project_kernel, in_specs=[hbm, hbm], out_specs=pl.BlockSpe...  7.27 us
    ppermute x3, waiting for transfers between devices, swap_tensor(): return lax.ppermute(value, 'tensor', [(i, i ^ k) for i in range(RING)])  4.49 us
    all_to_all x1, starting transfers between devices, on_device(): pieces = lax.all_to_all(attended, 'tensor', 0, 0)  4.29 us
    ppermute x3, starting transfers between devices, swap_tensor(): return lax.ppermute(value, 'tensor', [(i, i ^ k) for i in range(RING)])  4.12 us
    pallas_call x1, Pallas kernels, up(): pl.pallas_call(functools.partial(up_kernel, columns), in_specs=[vmem] * (...  1.88 us
  transfers between devices with their start and end apart: 17, of which 8 were waited for; matrix products, arithmetic and copies ran while one was open for 0% of the time, Pallas kernels for 27%

profile of v5, /device:TPU:0, one launch (start us, length us, event | category | flops | bytes accessed | tf_op | source)
XLA Modules:
  0.0 62.8 jit_solution(864261752073848079)
XLA Ops:
  0.0 1.0 %pad_maximum_fusion.refs_4_ = bf16[64,3072]{1,0:T(8,128)(2,1)S(1)} fusion(bf16[64,2048]{1,0:T(8,128)(2,1)} %bitcast.3, bf16[64,1024]{1,0:T(8,128)(2,1)} %bitcast.4), kind=kLoop, calls=%fused_computation.9 | loop fusion | flops 786432 | bytes 786432 | tf_op jit(solution)/shard_map/concatenate | solution.py:348
  1.1 4.2 %collective-permute-start.1 = (bf16[64,3072]{1,0:T(8,128)(2,1)S(1)}, bf16[64,3072]{1,0:T(8,128)(2,1)}, u32[]{:S(2)}, u32[]{:S(2)}) collective-permute-start(bf16[64,3072]{1,0:T(8,128)(2,1)S(1)} %pad_maximum_fusion.refs_4_), channel_id=1, source_target_pairs={{0,24},{4,28},{8,16},{12,20},{16,8},{20,12},{24,0},{28,4},{32,56},... | collective-permute-start | bytes 1179656 | tf_op jit(solution)/shard_map/ppermute | solution.py:313
  5.3 8.4 %shard_map.109 = (bf16[4,128,1024]{2,1,0:T(8,128)(2,1)}, bf16[64,1024]{1,0:T(8,128)(2,1)}, bf16[64,1024]{1,0:T(8,128)(2,1)}, bf16[64,1024]{1,0:T(8,128)(2,1)}, bf16[64,1024]{1,0:T(8,128)(2,1)}) custom-call(s32[128]{0:T(128)} %refs_0_.1, s32[32]{0:T(128)} %refs_1_.1, s32[1,128]{1,0:T(1,128)} %bitcast.5, bf16[128,1024]{1,0:T(8,128)(2,1)} %refs_3_.1, ...), custom_call_target="tpu_custom_call" | custom-call | flops 134217728 | bytes 16777216 | tf_op jit(solution)/shard_map/pallas_call | solution.py:145
  13.8 1.6 %collective-permute-start.6 = (bf16[64,3072]{1,0:T(8,128)(2,1)S(1)}, bf16[64,3072]{1,0:T(8,128)(2,1)S(1)}, u32[]{:S(2)}, u32[]{:S(2)}) collective-permute-start(bf16[64,3072]{1,0:T(8,128)(2,1)S(1)} %pad_maximum_fusion.refs_4_), channel_id=1, source_target_pairs={{0,16},{4,20},{8,24},{12,28},{16,0},{20,4},{24,8},{28,12},{32,48},... | collective-permute-start | bytes 1179656 | tf_op jit(solution)/shard_map/ppermute | solution.py:313
  15.4 4.3 %all-to-all-start = ((bf16[4,128,1024]{2,1,0:T(8,128)(2,1)}), bf16[4,128,1024]{2,1,0:T(8,128)(2,1)}, u32[]{:S(2)}, u32[]{:S(2)}) async-start(bf16[4,128,1024]{2,1,0:T(8,128)(2,1)} %get-tuple-element.58), calls=%async_computation | async-start | bytes 2097152 | tf_op jit(solution)/shard_map/all_to_all | solution.py:363
  19.7 1.7 %collective-permute-start.3 = (bf16[64,1024]{1,0:T(8,128)(2,1)S(1)}, bf16[64,1024]{1,0:T(8,128)(2,1)S(1)}, u32[]{:S(2)}, u32[]{:S(2)}) collective-permute-start(bf16[64,1024]{1,0:T(8,128)(2,1)S(1)} %copy-done.5), channel_id=1, source_target_pairs={{0,32},{4,36},{8,40},{12,44},{16,48},{20,52},{24,56},{28,60},{32,0... | collective-permute-start | bytes 393224 | tf_op jit(solution)/shard_map/ppermute | solution.py:313
  21.4 2.9 %collective-permute-start.4 = (bf16[64,1024]{1,0:T(8,128)(2,1)S(1)}, bf16[64,1024]{1,0:T(8,128)(2,1)S(1)}, u32[]{:S(2)}, u32[]{:S(2)}) collective-permute-start(bf16[64,1024]{1,0:T(8,128)(2,1)S(1)} %copy-done.4), channel_id=1, source_target_pairs={{0,64},{4,68},{8,72},{12,76},{16,80},{20,84},{24,88},{28,92},{32,9... | collective-permute-start | bytes 393224 | tf_op jit(solution)/shard_map/ppermute | solution.py:313
  24.5 2.0 %collective-permute-done.6.refs_8_ = bf16[64,3072]{1,0:T(8,128)(2,1)S(1)} collective-permute-done((bf16[64,3072]{1,0:T(8,128)(2,1)S(1)}, bf16[64,3072]{1,0:T(8,128)(2,1)S(1)}, u32[]{:S(2)}, u32[]{:S(2)}) %collective-permute-start.6) | collective-permute-done | bytes 393248 | tf_op jit(solution)/shard_map/ppermute | solution.py:313
  26.5 3.8 %collective-permute-done.4.refs_2_ = bf16[64,1024]{1,0:T(8,128)(2,1)S(1)} collective-permute-done((bf16[64,1024]{1,0:T(8,128)(2,1)S(1)}, bf16[64,1024]{1,0:T(8,128)(2,1)S(1)}, u32[]{:S(2)}, u32[]{:S(2)}) %collective-permute-start.4) | collective-permute-done | bytes 131104 | tf_op jit(solution)/shard_map/ppermute | solution.py:313
  30.3 2.0 %collective-permute-done.5.refs_3_ = bf16[64,1024]{1,0:T(8,128)(2,1)S(1)} collective-permute-done((bf16[64,1024]{1,0:T(8,128)(2,1)S(1)}, bf16[64,1024]{1,0:T(8,128)(2,1)S(1)}, u32[]{:S(2)}, u32[]{:S(2)}) %collective-permute-start.5) | collective-permute-done | bytes 131104 | tf_op jit(solution)/shard_map/ppermute | solution.py:313
  32.4 1.6 %collective-permute-done.8.refs_9_ = bf16[64,3072]{1,0:T(8,128)(2,1)S(1)} collective-permute-done((bf16[64,3072]{1,0:T(8,128)(2,1)S(1)}, bf16[64,3072]{1,0:T(8,128)(2,1)S(1)}, u32[]{:S(2)}, u32[]{:S(2)}) %collective-permute-start.8) | collective-permute-done | bytes 393248 | tf_op jit(solution)/shard_map/ppermute | solution.py:313
  34.0 1.6 %shard_map.110.refs_0_ = f32[128,128]{1,0:T(8,128)S(1)} custom-call(bf16[64,1024]{1,0:T(8,128)(2,1)S(1)} %copy-done, bf16[64,1024]{1,0:T(8,128)(2,1)S(1)} %collective-permute-done.3.refs_1_, bf16[64,1024]{1,0:T(8,128)(2,1)S(1)} %collective-permute-done.4.refs_2_, bf16[64,1024]{1,0:T(8,128)(2,1)S(1)} %collective-permute-done.5.refs_3_, ...), custom_call_target="tpu_custom_call" | custom-call | tf_op jit(solution)/shard_map/pallas_call | solution.py:206
  35.7 2.7 %collective-permute-start.12 = (f32[128,128]{1,0:T(8,128)S(1)}, f32[128,128]{1,0:T(8,128)S(1)}, u32[]{:S(2)}, u32[]{:S(2)}) collective-permute-start(f32[128,128]{1,0:T(8,128)S(1)} %shard_map.110.refs_0_), channel_id=1, source_target_pairs={{0,3},{1,2},{2,1},{3,0},{4,7},{5,6},{6,5},{7,4},{8,11},{9,10},{10,... | collective-permute-start | bytes 196616 | tf_op jit(solution)/shard_map/ppermute | solution.py:309
  38.4 0.8 %collective-permute-start.11 = (f32[128,128]{1,0:T(8,128)S(1)}, f32[128,128]{1,0:T(8,128)S(1)}, u32[]{:S(2)}, u32[]{:S(2)}) collective-permute-start(f32[128,128]{1,0:T(8,128)S(1)} %shard_map.110.refs_0_), channel_id=1, source_target_pairs={{0,2},{1,3},{2,0},{3,1},{4,6},{5,7},{6,4},{7,5},{8,10},{9,11},{10,... | collective-permute-start | bytes 196616 | tf_op jit(solution)/shard_map/ppermute | solution.py:309
  39.2 0.5 collective-permute-start.10
  40.0 1.2 %collective-permute-done.12.refs_3_ = f32[128,128]{1,0:T(8,128)S(1)} collective-permute-done((f32[128,128]{1,0:T(8,128)S(1)}, f32[128,128]{1,0:T(8,128)S(1)}, u32[]{:S(2)}, u32[]{:S(2)}) %collective-permute-start.12) | collective-permute-done | bytes 65568 | tf_op jit(solution)/shard_map/ppermute | solution.py:309
  41.2 3.3 %collective-permute-done.11.refs_2_ = f32[128,128]{1,0:T(8,128)S(1)} collective-permute-done((f32[128,128]{1,0:T(8,128)S(1)}, f32[128,128]{1,0:T(8,128)S(1)}, u32[]{:S(2)}, u32[]{:S(2)}) %collective-permute-start.11) | collective-permute-done | bytes 65568 | tf_op jit(solution)/shard_map/ppermute | solution.py:309
  44.4 1.9 %shard_map.112 = (bf16[64,2048]{1,0:T(8,128)(2,1)S(1)}, bf16[64,2048]{1,0:T(8,128)(2,1)S(1)}, bf16[64,2048]{1,0:T(8,128)(2,1)S(1)}, bf16[64,2048]{1,0:T(8,128)(2,1)S(1)}) custom-call(f32[128,128]{1,0:T(8,128)S(1)} %shard_map.110.refs_0_, f32[128,128]{1,0:T(8,128)S(1)} %collective-permute-done.10.refs_1_, f32[128,128]{1,0:T(8,128)S(1)} %collective-permute-done.11.refs_2_, ...), custom_call_target="tpu_custom_call" | custom-call | tf_op jit(solution)/shard_map/pallas_call | solution.py:245
  46.4 2.3 %collective-permute-start.14 = (bf16[64,2048]{1,0:T(8,128)(2,1)S(1)}, bf16[64,2048]{1,0:T(8,128)(2,1)S(1)}, u32[]{:S(2)}, u32[]{:S(2)}) collective-permute-start(bf16[64,2048]{1,0:T(8,128)(2,1)S(1)} %get-tuple-element.67), channel_id=1, source_target_pairs={{0,64},{4,68},{8,72},{12,76},{16,80},{20,84},{24,88},{28,92},{32,9... | collective-permute-start | bytes 786440 | tf_op jit(solution)/shard_map/ppermute | solution.py:313
  48.7 2.4 %collective-permute-start.15 = (bf16[64,2048]{1,0:T(8,128)(2,1)S(1)}, bf16[64,2048]{1,0:T(8,128)(2,1)S(1)}, u32[]{:S(2)}, u32[]{:S(2)}) collective-permute-start(bf16[64,2048]{1,0:T(8,128)(2,1)S(1)} %get-tuple-element.68), channel_id=1, source_target_pairs={{0,96},{4,100},{8,104},{12,108},{16,112},{20,116},{24,120},{28,124... | collective-permute-start | bytes 786440 | tf_op jit(solution)/shard_map/ppermute | solution.py:313
  51.1 7.3 %shard_map.111 = f32[128,2048]{1,0:T(8,128)S(1)} custom-call(bf16[4,128,1024]{2,1,0:T(8,128)(2,1)} %all-to-all-done.piece_hbm, bf16[4096,2048]{1,0:T(8,128)(2,1)} %weight_hbm.1), custom_call_target="tpu_custom_call" | custom-call | flops 2147483648 | bytes 16777216 | tf_op jit(solution)/shard_map/pallas_call | solution.py:288
  58.4 0.6 collective-permute-done.14
  59.0 2.6 %collective-permute-done.15 = bf16[64,2048]{1,0:T(8,128)(2,1)S(1)} collective-permute-done((bf16[64,2048]{1,0:T(8,128)(2,1)S(1)}, bf16[64,2048]{1,0:T(8,128)(2,1)S(1)}, u32[]{:S(2)}, u32[]{:S(2)}) %collective-permute-start.15) | collective-permute-done | bytes 262176 | tf_op jit(solution)/shard_map/ppermute | solution.py:313
  61.9 0.9 %add_convert_fusion = bf16[128,2048]{1,0:T(8,128)(2,1)} fusion(f32[128,2048]{1,0:T(8,128)S(1)} %shard_map.111, f32[128,2048]{1,0:T(8,128)S(1)} %fusion), kind=kLoop, calls=%fused_computation.8 | loop fusion | flops 524288 | bytes 2621440 | tf_op jit(solution)/shard_map/convert_element_type | solution.py:393
  (32 shorter events, 1.1 us)
Async XLA Ops:
  1.0 18.7 %collective-permute-start.2 = (bf16[64,3072]{1,0:T(8,128)(2,1)S(1)}, bf16[64,3072]{1,0:T(8,128)(2,1)S(1)}, u32[]{:S(2)}, u32[]{:S(2)}) collective-permute-start(bf16[64,3072]{1,0:T(8,128)(2,1)S(1)} %pad_maximum_fusion.refs_4_), channel_id=1, source_target_pairs={{0,4},{4,0},{8,12},{12,8},{16,20},{20,16},{24,28},{28,24},{32,36},... | collective-permute-start | bytes 1179656 | tf_op jit(solution)/shard_map/ppermute | solution.py:313
  1.1 18.6 %collective-permute-start.1 = (bf16[64,3072]{1,0:T(8,128)(2,1)S(1)}, bf16[64,3072]{1,0:T(8,128)(2,1)}, u32[]{:S(2)}, u32[]{:S(2)}) collective-permute-start(bf16[64,3072]{1,0:T(8,128)(2,1)S(1)} %pad_maximum_fusion.refs_4_), channel_id=1, source_target_pairs={{0,24},{4,28},{8,16},{12,20},{16,8},{20,12},{24,0},{28,4},{32,56},... | collective-permute-start | bytes 1179656 | tf_op jit(solution)/shard_map/ppermute | solution.py:313
  5.3 14.4 %collective-permute-start = (bf16[64,3072]{1,0:T(8,128)(2,1)S(1)}, bf16[64,3072]{1,0:T(8,128)(2,1)}, u32[]{:S(2)}, u32[]{:S(2)}) collective-permute-start(bf16[64,3072]{1,0:T(8,128)(2,1)S(1)} %pad_maximum_fusion.refs_4_), channel_id=1, source_target_pairs={{0,8},{4,12},{8,0},{12,4},{16,24},{20,28},{24,16},{28,20},{32,40},... | collective-permute-start | bytes 1179656 | tf_op jit(solution)/shard_map/ppermute | solution.py:313
  13.7 6.0 %copy-start.5 = (bf16[64,1024]{1,0:T(8,128)(2,1)S(1)}, bf16[64,1024]{1,0:T(8,128)(2,1)}, u32[]{:S(2)}) copy-start(bf16[64,1024]{1,0:T(8,128)(2,1)} %get-tuple-element.46) | copy-start | bytes 393220
  13.7 7.7 %copy-start.4 = (bf16[64,1024]{1,0:T(8,128)(2,1)S(1)}, bf16[64,1024]{1,0:T(8,128)(2,1)}, u32[]{:S(2)}) copy-start(bf16[64,1024]{1,0:T(8,128)(2,1)} %get-tuple-element.47) | copy-start | bytes 393220
  13.7 10.6 %copy-start.3 = (bf16[64,1024]{1,0:T(8,128)(2,1)S(1)}, bf16[64,1024]{1,0:T(8,128)(2,1)}, u32[]{:S(2)}) copy-start(bf16[64,1024]{1,0:T(8,128)(2,1)} %get-tuple-element.48) | copy-start | bytes 393220
  13.7 18.6 %copy-start.1 = (s32[32]{0:T(128)S(1)}, s32[32]{0:T(128)}, u32[]{:S(2)}) copy-start(s32[32]{0:T(128)} %refs_1_.1) | copy-start | bytes 388
  13.8 18.6 %copy-start.2 = (s32[128]{0:T(128)S(1)}, s32[128]{0:T(128)}, u32[]{:S(2)}) copy-start(s32[128]{0:T(128)} %param.18) | copy-start | bytes 1540
  13.8 20.3 %copy-start = (bf16[64,1024]{1,0:T(8,128)(2,1)S(1)}, bf16[64,1024]{1,0:T(8,128)(2,1)}, u32[]{:S(2)}) copy-start(bf16[64,1024]{1,0:T(8,128)(2,1)} %get-tuple-element.50.refs_0_) | copy-start | bytes 393220
  13.8 12.8 %collective-permute-start.6 = (bf16[64,3072]{1,0:T(8,128)(2,1)S(1)}, bf16[64,3072]{1,0:T(8,128)(2,1)S(1)}, u32[]{:S(2)}, u32[]{:S(2)}) collective-permute-start(bf16[64,3072]{1,0:T(8,128)(2,1)S(1)} %pad_maximum_fusion.refs_4_), channel_id=1, source_target_pairs={{0,16},{4,20},{8,24},{12,28},{16,0},{20,4},{24,8},{28,12},{32,48},... | collective-permute-start | bytes 1179656 | tf_op jit(solution)/shard_map/ppermute | solution.py:313
  15.4 24.5 %all-to-all-start = ((bf16[4,128,1024]{2,1,0:T(8,128)(2,1)}), bf16[4,128,1024]{2,1,0:T(8,128)(2,1)}, u32[]{:S(2)}, u32[]{:S(2)}) async-start(bf16[4,128,1024]{2,1,0:T(8,128)(2,1)} %get-tuple-element.58), calls=%async_computation | async-start | bytes 2097152 | tf_op jit(solution)/shard_map/all_to_all | solution.py:363
  19.7 6.8 %collective-permute-start.3 = (bf16[64,1024]{1,0:T(8,128)(2,1)S(1)}, bf16[64,1024]{1,0:T(8,128)(2,1)S(1)}, u32[]{:S(2)}, u32[]{:S(2)}) collective-permute-start(bf16[64,1024]{1,0:T(8,128)(2,1)S(1)} %copy-done.5), channel_id=1, source_target_pairs={{0,32},{4,36},{8,40},{12,44},{16,48},{20,52},{24,56},{28,60},{32,0... | collective-permute-start | bytes 393224 | tf_op jit(solution)/shard_map/ppermute | solution.py:313
  21.4 8.9 %collective-permute-start.4 = (bf16[64,1024]{1,0:T(8,128)(2,1)S(1)}, bf16[64,1024]{1,0:T(8,128)(2,1)S(1)}, u32[]{:S(2)}, u32[]{:S(2)}) collective-permute-start(bf16[64,1024]{1,0:T(8,128)(2,1)S(1)} %copy-done.4), channel_id=1, source_target_pairs={{0,64},{4,68},{8,72},{12,76},{16,80},{20,84},{24,88},{28,92},{32,9... | collective-permute-start | bytes 393224 | tf_op jit(solution)/shard_map/ppermute | solution.py:313
  24.3 8.0 %collective-permute-start.5 = (bf16[64,1024]{1,0:T(8,128)(2,1)S(1)}, bf16[64,1024]{1,0:T(8,128)(2,1)S(1)}, u32[]{:S(2)}, u32[]{:S(2)}) collective-permute-start(bf16[64,1024]{1,0:T(8,128)(2,1)S(1)} %copy-done.3), channel_id=1, source_target_pairs={{0,96},{4,100},{8,104},{12,108},{16,112},{20,116},{24,120},{28,124... | collective-permute-start | bytes 393224 | tf_op jit(solution)/shard_map/ppermute | solution.py:313
  24.5 7.9 %collective-permute-start.7 = (bf16[64,3072]{1,0:T(8,128)(2,1)}, bf16[64,3072]{1,0:T(8,128)(2,1)S(1)}, u32[]{:S(2)}, u32[]{:S(2)}) collective-permute-start(bf16[64,3072]{1,0:T(8,128)(2,1)} %collective-permute-done.refs_6_), channel_id=1, source_target_pairs={{0,4},{4,0},{8,12},{12,8},{16,20},{20,16},{24,28},{28,24},{32,36},... | collective-permute-start | bytes 1179656 | tf_op jit(solution)/shard_map/ppermute | solution.py:313
  26.5 5.9 %collective-permute-start.9 = (bf16[64,3072]{1,0:T(8,128)(2,1)}, bf16[64,3072]{1,0:T(8,128)(2,1)S(1)}, u32[]{:S(2)}, u32[]{:S(2)}) collective-permute-start(bf16[64,3072]{1,0:T(8,128)(2,1)} %collective-permute-done.1.refs_10_), channel_id=1, source_target_pairs={{0,4},{4,0},{8,12},{12,8},{16,20},{20,16},{24,28},{28,24},{32,36},... | collective-permute-start | bytes 1179656 | tf_op jit(solution)/shard_map/ppermute | solution.py:313
  32.3 1.7 %collective-permute-start.8 = (bf16[64,3072]{1,0:T(8,128)(2,1)S(1)}, bf16[64,3072]{1,0:T(8,128)(2,1)S(1)}, u32[]{:S(2)}, u32[]{:S(2)}) collective-permute-start(bf16[64,3072]{1,0:T(8,128)(2,1)S(1)} %collective-permute-done.6.refs_8_), channel_id=1, source_target_pairs={{0,4},{4,0},{8,12},{12,8},{16,20},{20,16},{24,28},{28,24},{32,36},... | collective-permute-start | bytes 1179656 | tf_op jit(solution)/shard_map/ppermute | solution.py:313
  35.7 5.5 %collective-permute-start.12 = (f32[128,128]{1,0:T(8,128)S(1)}, f32[128,128]{1,0:T(8,128)S(1)}, u32[]{:S(2)}, u32[]{:S(2)}) collective-permute-start(f32[128,128]{1,0:T(8,128)S(1)} %shard_map.110.refs_0_), channel_id=1, source_target_pairs={{0,3},{1,2},{2,1},{3,0},{4,7},{5,6},{6,5},{7,4},{8,11},{9,10},{10,... | collective-permute-start | bytes 196616 | tf_op jit(solution)/shard_map/ppermute | solution.py:309
  38.4 6.1 %collective-permute-start.11 = (f32[128,128]{1,0:T(8,128)S(1)}, f32[128,128]{1,0:T(8,128)S(1)}, u32[]{:S(2)}, u32[]{:S(2)}) collective-permute-start(f32[128,128]{1,0:T(8,128)S(1)} %shard_map.110.refs_0_), channel_id=1, source_target_pairs={{0,2},{1,3},{2,0},{3,1},{4,6},{5,7},{6,4},{7,5},{8,10},{9,11},{10,... | collective-permute-start | bytes 196616 | tf_op jit(solution)/shard_map/ppermute | solution.py:309
  39.2 5.2 %collective-permute-start.10 = (f32[128,128]{1,0:T(8,128)S(1)}, f32[128,128]{1,0:T(8,128)S(1)}, u32[]{:S(2)}, u32[]{:S(2)}) collective-permute-start(f32[128,128]{1,0:T(8,128)S(1)} %shard_map.110.refs_0_), channel_id=1, source_target_pairs={{0,1},{1,0},{2,3},{3,2},{4,5},{5,4},{6,7},{7,6},{8,9},{9,8},{10,11... | collective-permute-start | bytes 196616 | tf_op jit(solution)/shard_map/ppermute | solution.py:309
  46.3 12.1 %collective-permute-start.13 = (bf16[64,2048]{1,0:T(8,128)(2,1)S(1)}, bf16[64,2048]{1,0:T(8,128)(2,1)S(1)}, u32[]{:S(2)}, u32[]{:S(2)}) collective-permute-start(bf16[64,2048]{1,0:T(8,128)(2,1)S(1)} %get-tuple-element.66), channel_id=1, source_target_pairs={{0,32},{4,36},{8,40},{12,44},{16,48},{20,52},{24,56},{28,60},{32,0... | collective-permute-start | bytes 786440 | tf_op jit(solution)/shard_map/ppermute | solution.py:313
  46.4 12.6 %collective-permute-start.14 = (bf16[64,2048]{1,0:T(8,128)(2,1)S(1)}, bf16[64,2048]{1,0:T(8,128)(2,1)S(1)}, u32[]{:S(2)}, u32[]{:S(2)}) collective-permute-start(bf16[64,2048]{1,0:T(8,128)(2,1)S(1)} %get-tuple-element.67), channel_id=1, source_target_pairs={{0,64},{4,68},{8,72},{12,76},{16,80},{20,84},{24,88},{28,92},{32,9... | collective-permute-start | bytes 786440 | tf_op jit(solution)/shard_map/ppermute | solution.py:313
  48.7 12.9 %collective-permute-start.15 = (bf16[64,2048]{1,0:T(8,128)(2,1)S(1)}, bf16[64,2048]{1,0:T(8,128)(2,1)S(1)}, u32[]{:S(2)}, u32[]{:S(2)}) collective-permute-start(bf16[64,2048]{1,0:T(8,128)(2,1)S(1)} %get-tuple-element.68), channel_id=1, source_target_pairs={{0,96},{4,100},{8,104},{12,108},{16,112},{20,116},{24,120},{28,124... | collective-permute-start | bytes 786440 | tf_op jit(solution)/shard_map/ppermute | solution.py:313
